TPU v7x, 512 devices: a whole 4x4x16 slice. The times are simulated.
512 devices in a mesh: table: 32 (over z, core), ctx: 16 (over y, x).
Axes of the slice: x: 4, y: 4, z: 16, core: 2. Of those that a mesh axis runs over, the one named last changes fastest.
Arguments:
- item_ids: int32 [32, 2048], P('table', 'ctx'), may hold values from 0 to 16383, as said below
- history_len: int32 [32], P('table'), may hold values from 1 to 2048, 40960 in all
- item_slot: int32 [16384], replicated, may hold values from 0 to 16383, as said below
- table_slab: float32 [16384, 512], P('table'), may hold values from -20 to 20
- proj_in: bfloat16 [512, 2048], replicated, may hold values from -0.25 to 0.25
- proj_out: bfloat16 [512, 512], replicated, may hold values from -0.25 to 0.25
- upstream: bfloat16 [32, 2048, 512], P('table', 'ctx'), may hold values from -6 to 6
Outputs:
- layer_out: bfloat16 [32, 2048, 512], P('table', 'ctx')
- table_grad: float32 [16384, 512], P(('table', 'ctx'))
Inputs may be any that keep to these rules, and one draw needn't show every extreme that they name: `item_slot`: A permutation of the slots; slot s is row s % 512 of table shard s // 512. `item_ids`: in each aligned block of 128 event slots of one history (the events of one device), at most 12 items have their slot on any one table shard, and exactly 12 on some shard.
All inputs are finite; a program needn't handle non-finite values. No bound on the sum of `history_len` on one device may be relied on, other than what follows from the above.
Results may differ from a plain program's by a relative error of at most 0.013.
Values may be sent and summed in bfloat16 or wider, within the bound.
No kernel may reach another device: no remote copies, remote signals or barrier semaphores. Data moves between devices by JAX's collectives and lax.ppermute only.
A program may use at most 128 MiB of HBM per device.

v0:
```python
import jax
import jax.numpy as jnp
from jax import lax
from jax.sharding import PartitionSpec as P

HEAD_DIM = 128


EPSILON = 1e-05


def normalize(values):
    centre = values - jnp.mean(values, axis=-1, keepdims=True)
    scale_inv = lax.rsqrt(jnp.mean(centre * centre, axis=-1, keepdims=True) + EPSILON)
    return (centre * scale_inv, scale_inv)


def norm_back(grad, normed, scale_inv):
    return scale_inv * (
        grad
        - jnp.mean(grad, axis=-1, keepdims=True)
        - normed * jnp.mean(grad * normed, axis=-1, keepdims=True)
    )


def silu_slope(values):
    sig = jax.nn.sigmoid(values)
    return sig * (1.0 + values * (1.0 - sig))


def local(item_ids, history_len, item_slot, table_slab, proj_in, proj_out, upstream):
    tables = lax.axis_size("table")
    groups = lax.axis_size("ctx")
    ctx_index = lax.axis_index("ctx")
    block_len = item_ids.shape[1]
    shard_rows = table_slab.shape[0]
    row_width = table_slab.shape[1]
    capacity = 3 * block_len // tables
    width = proj_out.shape[0]
    head_count = width // HEAD_DIM
    seq_len = block_len * groups
    score_scale = HEAD_DIM ** (-0.5)
    slots = item_slot[item_ids[0]]
    owners = slots // shard_rows
    local_rows = slots % shard_rows
    owner_hits = (owners[:, None] == jnp.arange(tables)[None, :]).astype(jnp.int32)
    ranking = jnp.sum((jnp.cumsum(owner_hits, axis=0) - owner_hits) * owner_hits, axis=1)
    placing = owners * capacity + ranking
    requests = (
        jnp.full((tables * capacity,), -1, jnp.int32)
        .at[placing]
        .set(local_rows)
        .reshape(tables, capacity)
    )
    asked = lax.all_to_all(requests, "table", split_axis=0, concat_axis=0, tiled=True)
    present = asked >= 0
    rows_out = table_slab[jnp.where(present, asked, 0)] * present[..., None].astype(jnp.float32)
    fetched = lax.all_to_all(rows_out, "table", split_axis=0, concat_axis=0, tiled=True)
    positions = ctx_index * block_len + jnp.arange(block_len)
    length = history_len[0]
    validity = (positions < length).astype(jnp.float32)
    embedded = fetched.reshape(tables * capacity, row_width)[placing] * validity[:, None]
    normed, inv_std = normalize(embedded)
    projected = jnp.dot(normed.astype(jnp.bfloat16), proj_in, preferred_element_type=jnp.float32)
    gate_part = projected[:, : 2 * width]
    features = jnp.concatenate([jax.nn.silu(gate_part), projected[:, 2 * width :]], axis=1).astype(
        jnp.bfloat16
    )
    gate_u = features[:, :width]
    values_own = features[:, width : 2 * width]
    queries = features[:, 2 * width : 3 * width]
    keys_own = features[:, 3 * width :]
    all_keys, all_values = (
        lax.all_gather(keys_own, "ctx", axis=0, tiled=True),
        lax.all_gather(values_own, "ctx", axis=0, tiled=True),
    )
    query_heads = queries.reshape(block_len, head_count, HEAD_DIM)
    key_heads = all_keys.reshape(seq_len, head_count, HEAD_DIM)
    value_heads = all_values.reshape(seq_len, head_count, HEAD_DIM)
    key_pos = jnp.arange(seq_len)
    allowed = ((key_pos[None, :] <= positions[:, None]) & (key_pos[None, :] < length)).astype(
        jnp.float32
    )
    scores = (
        jnp.einsum("qhd,khd->hqk", query_heads, key_heads, preferred_element_type=jnp.float32)
        * score_scale
    )
    weights = (jax.nn.silu(scores) * allowed[None]).astype(jnp.bfloat16)
    attended = jnp.einsum(
        "hqk,khd->qhd", weights, value_heads, preferred_element_type=jnp.float32
    ).reshape(block_len, width)
    att_hat, att_inv = normalize(attended)
    gated = (att_hat * gate_u).astype(jnp.bfloat16)
    layer_out = (
        (embedded + jnp.dot(gated, proj_out, preferred_element_type=jnp.float32))
        * validity[:, None]
    ).astype(jnp.bfloat16)
    d_out = upstream[0] * validity[:, None].astype(jnp.bfloat16)
    d_gated = jnp.dot(d_out, proj_out.T, preferred_element_type=jnp.float32)
    d_gate = d_gated * att_hat
    d_attn = norm_back(d_gated * gate_u, att_hat, att_inv).astype(jnp.bfloat16)
    d_heads = d_attn.reshape(block_len, head_count, HEAD_DIM)
    d_weights = jnp.einsum("qhd,khd->hqk", d_heads, value_heads, preferred_element_type=jnp.float32)
    d_scores = (d_weights * silu_slope(scores) * allowed[None] * score_scale).astype(jnp.bfloat16)
    d_query = jnp.einsum(
        "hqk,khd->qhd", d_scores, key_heads, preferred_element_type=jnp.float32
    ).reshape(block_len, width)
    key_own_heads = keys_own.reshape(block_len, head_count, HEAD_DIM)
    value_own_heads = values_own.reshape(block_len, head_count, HEAD_DIM)
    zeros_acc = jnp.zeros((block_len, width), jnp.float32)
    piece_query = lax.all_gather(queries, "ctx", axis=0, tiled=True)
    piece_grad = lax.all_gather(d_attn, "ctx", axis=0, tiled=True)
    rows_in = piece_query.shape[0]
    query_pos = jnp.arange(rows_in)

    def compute(totals):
        piece_qh = piece_query.reshape(rows_in, head_count, HEAD_DIM)
        piece_dh = piece_grad.reshape(rows_in, head_count, HEAD_DIM)
        piece_scores = (
            jnp.einsum("qhd,khd->hqk", piece_qh, key_own_heads, preferred_element_type=jnp.float32)
            * score_scale
        )
        piece_allowed = (
            (positions[None, :] <= query_pos[:, None]) & (positions[None, :] < length)
        ).astype(jnp.float32)
        piece_weights = (jax.nn.silu(piece_scores) * piece_allowed[None]).astype(jnp.bfloat16)
        piece_dw = jnp.einsum(
            "qhd,khd->hqk", piece_dh, value_own_heads, preferred_element_type=jnp.float32
        )
        piece_ds = (piece_dw * silu_slope(piece_scores) * piece_allowed[None] * score_scale).astype(
            jnp.bfloat16
        )
        new_key = jnp.einsum(
            "hqk,qhd->khd", piece_ds, piece_qh, preferred_element_type=jnp.float32
        ).reshape(block_len, width)
        new_value = jnp.einsum(
            "hqk,qhd->khd", piece_weights, piece_dh, preferred_element_type=jnp.float32
        ).reshape(block_len, width)
        return (new_key, new_value)

    d_key, d_value = lax.cond(
        jnp.int32(0) + rows_in > positions[0],
        compute,
        lambda totals: totals,
        (zeros_acc, zeros_acc),
    )
    d_proj = jnp.concatenate(
        [jnp.concatenate([d_gate, d_value], axis=1) * silu_slope(gate_part), d_query, d_key], axis=1
    ).astype(jnp.bfloat16)
    d_normed = jnp.dot(d_proj, proj_in.T, preferred_element_type=jnp.float32)
    d_embedded = (d_out.astype(jnp.float32) + norm_back(d_normed, normed, inv_std)) * validity[
        :, None
    ]
    outgoing = (
        jnp.zeros((tables * capacity, row_width), jnp.float32)
        .at[placing]
        .set(d_embedded)
        .reshape(tables, capacity, row_width)
    )
    arrived = lax.all_to_all(
        outgoing.astype(jnp.bfloat16), "table", split_axis=0, concat_axis=0, tiled=True
    ).astype(outgoing.dtype)
    present = asked >= 0
    shard_sums = (
        jnp.zeros((shard_rows, row_width), jnp.float32)
        .at[jnp.where(present, asked, 0).reshape(-1)]
        .add((arrived * present[..., None].astype(jnp.float32)).reshape(-1, row_width))
    )
    table_grad = lax.psum_scatter(
        shard_sums.astype(jnp.bfloat16), "ctx", scatter_dimension=0, tiled=True
    ).astype(jnp.float32)
    return (layer_out[None], table_grad)


def solution(mesh):
    placed = (
        P("table", "ctx"),
        P("table"),
        P(),
        P("table", None),
        P(),
        P(),
        P("table", "ctx", None),
    )
    return jax.shard_map(
        local,
        mesh=mesh,
        in_specs=placed,
        out_specs=(P("table", "ctx", None), P(("table", "ctx"), None)),
        check_vma=False,
    )
```

profile of v0, /device:TPU:1, one launch (start us, length us, event | category | flops | bytes accessed | tf_op | source)
XLA Modules:
  0.0 522.5 jit_solution(4887679226383872522)
XLA Ops:
  11.3 28.3 %all_to_all.25 = s32[32,1,12]{2,1,0:T(1,128)S(1)} all-to-all(s32[32,1,12]{2,1,0:T(1,128)S(1)} %bitcast.146), channel_id=1, replica_groups=mesh['table'=32,'ctx'=16] {'table'}, dimensions={0} | all-to-all | bytes 3072 | tf_op jit(solution)/shard_map/all_to_all | solution.py:55
  39.8 3.2 gather_fusion.1
  44.8 2.4 broadcast_multiply_fusion
  47.2 5.2 all-to-all-start.1
  53.7 54.6 %all-to-all-done.1 = f32[32,12,512]{2,1,0:T(8,128)} async-done(((f32[32,12,512]{2,1,0:T(8,128)}), f32[32,12,512]{2,1,0:T(8,128)}, u32[]{:S(2)}, u32[]{:S(2)}) %all-to-all-start.1) | async-done | bytes 786464 | tf_op jit(solution)/shard_map/all_to_all | solution.py:58
  116.2 47.1 %all-gather.7.cloned.1.call-done = bf16[2048,512]{1,0:T(8,128)(2,1)} async-done(((bf16[128,512]{1,0:T(8,128)(2,1)}), bf16[2048,512]{1,0:T(8,128)(2,1)}) %all-gather.7.cloned.1.call-update) | async-done | bytes 2097168 | tf_op jit(solution)/shard_map/all_gather | solution.py:74
  163.3 3.9 copy.57
  167.2 4.2 fusion.68
  171.4 54.6 %all-gather.5.cloned.1.call-done = bf16[2048,512]{1,0:T(8,128)(2,1)} async-done(((bf16[128,512]{1,0:T(8,128)(2,1)}), bf16[2048,512]{1,0:T(8,128)(2,1)}) %all-gather.5.cloned.1.call-update) | async-done | bytes 2097168 | tf_op jit(solution)/shard_map/all_gather | solution.py:75
  226.0 6.1 %fusion.101 = (f32[128]{0:T(128)}, f32[4,128,128]{2,1,0:T(8,128)}) fusion(f32[4,128,2048]{2,1,0:T(8,128)} %fusion.68, f32[128,2048]{1,0:T(8,128)} %fusion.37, bf16[2048,512]{1,0:T(8,128)(2,1)} %all-gather.5.cloned.1.call-done), kind=kOutput, calls=%fused_computation.154 | convolution fusion | flops 275840896 | bytes 7602688 | tf_op jit(solution)/shard_map/hqk,khd->qhd/dot_general | solution.py:89
  239.7 7.1 %fusion.32 = bf16[4,128,128]{2,1,0:T(8,128)(2,1)} fusion(bf16[2048,4,128]{0,2,1:T(8,128)(2,1)} %bitcast.136, f32[4,128,2048]{2,1,0:T(8,128)} %fusion.68, f32[128,2048]{1,0:T(8,128)} %fusion.37, bf16[2048,512]{1,0:T(8,128)(2,1)} %all-gather.5.cloned.1.call-done, bf16[128,512]{1,0:T(8,128)(2,1)} %get-tuple-element.60), kind=kOutput, calls=%fused_computation.39 | convolution fusion | flops 549519360 | bytes 9699328 | tf_op jit(solution)/shard_map/hqk,khd->qhd/dot_general | solution.py:105
  248.5 40.8 %all-gather.11.cloned.1.call-done = bf16[2048,512]{1,0:T(8,128)(2,1)} async-done(((bf16[128,512]{1,0:T(8,128)(2,1)}), bf16[2048,512]{1,0:T(8,128)(2,1)}) %all-gather.11.cloned.1.call-update) | async-done | bytes 2097168 | tf_op jit(solution)/shard_map/all_gather | solution.py:111
  289.3 62.6 %all-gather.9.cloned.1.call-done = bf16[2048,512]{1,0:T(8,128)(2,1)} async-done(((bf16[128,512]{1,0:T(8,128)(2,1)}), bf16[2048,512]{1,0:T(8,128)(2,1)}) %all-gather.9.cloned.1.call-update) | async-done | bytes 2097168 | tf_op jit(solution)/shard_map/all_gather | solution.py:112
  352.0 26.1 %conditional.1 = (f32[128,512]{1,0:T(8,128)}, bf16[128,512]{1,0:T(8,128)(2,1)}) conditional(s32[]{:T(128)} %bitcast.18, () %tuple.16, (bf16[2048,512]{1,0:T(8,128)(2,1)}, bf16[128,512]{1,0:T(8,128)(2,1)}, bf16[2048,512]{1,0:T(8,128)(2,1)}, bf16[128,512]{1,0:T(8,128)(2,1)S(1)}, s32[128]{0:T(128)}, /*index=5*/s32[2048]{0:T(1024)S(1)}, ...), branch_computations={%region_9.10_spmd, %region_10.11_spmd} | conditional | flops 1094516864 | bytes 29762836 | solution.py:141
  353.2 1.9 and_convert_fusion
  355.1 4.0 copy.43
  359.1 4.4 fusion.15
  363.5 6.3 %fusion.8 = bf16[4,128,128]{1,2,0:T(8,128)(2,1)S(1)} fusion(bf16[2048,4,128]{0,2,1:T(8,128)(2,1)} %bitcast.138, f32[4,2048,128]{2,1,0:T(8,128)} %fusion.15, f32[2048,128]{1,0:T(8,128)} %and_convert_fusion, bf16[2048,512]{1,0:T(8,128)(2,1)} %get-tuple-element.16, bf16[128,512]{1,0:T(8,128)(2,1)} %get-tuple-element.17), kind=kOutput, calls=%fused_computation.15 | convolution fusion | flops 549519360 | bytes 9699328 | tf_op jit(solution)/shard_map/cond/branch_1_fun/hqk,qhd->khd/dot_general | solution.py:133
  369.8 5.7 %fusion = f32[4,128,128]{1,2,0:T(8,128)} fusion(f32[4,2048,128]{2,1,0:T(8,128)} %fusion.15, f32[2048,128]{1,0:T(8,128)} %and_convert_fusion, bf16[2048,512]{1,0:T(8,128)(2,1)} %get-tuple-element.16), kind=kOutput, calls=%fused_computation.9 | convolution fusion | flops 275775488 | bytes 7602176 | tf_op jit(solution)/shard_map/cond/branch_1_fun/hqk,qhd->khd/dot_general | solution.py:136
  384.9 14.0 %all-to-all-start.2 = ((bf16[32,12,512]{2,1,0:T(8,128)(2,1)}), bf16[32,12,512]{2,1,0:T(8,128)(2,1)}, u32[]{:S(2)}, u32[]{:S(2)}) async-start(bf16[32,12,512]{2,1,0:T(8,128)(2,1)} %convert_element_type.118), calls=%async_computation.2 | async-start | bytes 1048576 | tf_op jit(solution)/shard_map/all_to_all | solution.py:160
  400.3 32.2 %all-to-all-done.2 = bf16[32,12,512]{2,1,0:T(8,128)(2,1)} async-done(((bf16[32,12,512]{2,1,0:T(8,128)(2,1)}), bf16[32,12,512]{2,1,0:T(8,128)(2,1)}, u32[]{:S(2)}, u32[]{:S(2)}) %all-to-all-start.2) | async-done | bytes 393248 | tf_op jit(solution)/shard_map/all_to_all | solution.py:160
  434.6 3.7 scatter_custom_fusion.2
  439.2 2.1 fusion.35
  441.4 73.2 %reduce-scatter.2.cloned.1.call-done = bf16[32,512]{1,0:T(8,128)(2,1)} async-done(((bf16[512,512]{1,0:T(8,128)(2,1)}), bf16[32,512]{1,0:T(8,128)(2,1)}) %reduce-scatter.2.cloned.1.call-update) | async-done | bytes 32784 | tf_op jit(solution)/shard_map/reduce_scatter | solution.py:169
  (99 shorter events, 39.4 us)
Async XLA Ops:
  7.2 103.5 %copy-start = (bf16[512,2048]{1,0:T(8,128)(2,1)S(1)}, bf16[512,2048]{1,0:T(8,128)(2,1)}, u32[]{:S(2)}) copy-start(bf16[512,2048]{1,0:T(8,128)(2,1)} %param.13) | copy-start | bytes 6291460
  10.2 43.4 %copy-start.15 = (s32[128]{0:T(128)}, s32[128]{0:T(128)S(1)}, u32[]{:S(2)}) copy-start(s32[128]{0:T(128)S(1)} %fusion.91) | copy-start | bytes 1540
  44.2 0.6 copy-start.5
  47.2 61.0 %all-to-all-start.1 = ((f32[32,12,512]{2,1,0:T(8,128)}), f32[32,12,512]{2,1,0:T(8,128)}, u32[]{:S(2)}, u32[]{:S(2)}) async-start(f32[32,12,512]{2,1,0:T(8,128)} %broadcast_multiply_fusion), calls=%async_computation.1 | async-start | bytes 2097152 | tf_op jit(solution)/shard_map/all_to_all | solution.py:58
  52.4 110.9 %all-gather.7.cloned.1.call-start = ((), (), s32[]{:S(2)}) async-start(), calls=%async_computation.5 | async-start | bytes 2228224 | tf_op jit(solution)/shard_map/all_gather | solution.py:74
  53.7 57.6 %copy-start.6 = (f32[128]{0:T(128)}, f32[128]{0:T(128)S(1)}, u32[]{:S(2)}) copy-start(f32[128]{0:T(128)S(1)} %get-tuple-element.58) | copy-start | bytes 1540
  110.5 0.8 copy-start.10
  110.7 0.6 copy-start.14
  112.0 114.0 %all-gather.5.cloned.1.call-start = ((), (), s32[]{:S(2)}) async-start(), calls=%async_computation.4 | async-start | bytes 2228224 | tf_op jit(solution)/shard_map/all_gather | solution.py:75
  112.2 0.7 copy-start.1
  113.6 175.7 %all-gather.11.cloned.1.call-start = ((), (), s32[]{:S(2)}) async-start(), calls=%async_computation.7 | async-start | bytes 2228224 | tf_op jit(solution)/shard_map/all_gather | solution.py:111
  114.4 237.6 %all-gather.9.cloned.1.call-start = ((), (), s32[]{:S(2)}) async-start(), calls=%async_computation.6 | async-start | bytes 2228224 | tf_op jit(solution)/shard_map/all_gather | solution.py:112
  114.4 0.5 copy-start.13
  171.4 64.2 %copy-start.3 = (bf16[1,128,512]{2,1,0:T(8,128)(2,1)S(1)}, bf16[1,128,512]{2,1,0:T(8,128)(2,1)}, u32[]{:S(2)}) copy-start(bf16[1,128,512]{2,1,0:T(8,128)(2,1)} %param.15) | copy-start | bytes 393220
  234.5 4.5 copy-start.8
  235.6 3.5 copy-start.11
  239.7 112.2 %copy-start.2 = (bf16[128,512]{1,0:T(8,128)(2,1)S(1)}, bf16[128,512]{1,0:T(8,128)(2,1)}, u32[]{:S(2)}) copy-start(bf16[128,512]{1,0:T(8,128)(2,1)} %get-tuple-element.63) | copy-start | bytes 393220
  378.0 4.2 copy-start.4
  384.9 54.3 %copy-start.7 = (f32[128]{0:T(128)S(1)}, f32[128]{0:T(128)}, u32[]{:S(2)}) copy-start(f32[128]{0:T(128)} %copy-done.6) | copy-start | bytes 1540
  384.9 54.3 %copy-start.9 = (f32[128]{0:T(128)S(1)}, f32[128]{0:T(128)}, u32[]{:S(2)}) copy-start(f32[128]{0:T(128)} %copy-done.8) | copy-start | bytes 1540
  384.9 54.3 %copy-start.12 = (f32[128]{0:T(128)S(1)}, f32[128]{0:T(128)}, u32[]{:S(2)}) copy-start(f32[128]{0:T(128)} %copy-done.11) | copy-start | bytes 1540
  384.9 47.6 %all-to-all-start.2 = ((bf16[32,12,512]{2,1,0:T(8,128)(2,1)}), bf16[32,12,512]{2,1,0:T(8,128)(2,1)}, u32[]{:S(2)}, u32[]{:S(2)}) async-start(bf16[32,12,512]{2,1,0:T(8,128)(2,1)} %convert_element_type.118), calls=%async_computation.2 | async-start | bytes 1048576 | tf_op jit(solution)/shard_map/all_to_all | solution.py:160
  398.9 115.7 %reduce-scatter.2.cloned.1.call-start = ((), (), s32[]{:S(2)}) async-start(), calls=%async_computation.8 | async-start | bytes 557056 | tf_op jit(solution)/shard_map/reduce_scatter | solution.py:169
Sparse Core Ops, SparseCore 0:
  112.2 51.0 all-gather.6
  166.3 59.6 all-gather.4
  229.6 59.6 all-gather.10
  292.2 59.6 all-gather.8
  439.3 75.2 reduce-scatter.1
where the time goes:
time: 524 us; the launch traced here: 523 us
  waiting for transfers between devices  366 us (70%)
  matrix products  40 us (8%)
  local copies, waits for them, and re-layouts  29 us (6%)
  blocking collectives  28.3 us (5%)
  other arithmetic  24.6 us (5%)
  starting transfers between devices  19.4 us (4%)
  between operations  15.4 us (3%)
    reduce_scatter x1, waiting for transfers between devices, local(): lax.psum_scatter(shard_sums.astype(jnp.bfloat16), 'ctx', scatter_dimensio...  73.2 us
    all_gather x1, waiting for transfers between devices, local(): piece_grad = lax.all_gather(d_attn, 'ctx', axis=0, tiled=True)  62.6 us
    all_gather x1, waiting for transfers between devices, local(): lax.all_gather(values_own, 'ctx', axis=0, tiled=True)  54.6 us
    all_to_all x1, waiting for transfers between devices, local(): lax.all_to_all(rows_out, 'table', split_axis=0, concat_axis=0, tiled=True)  54.6 us
    all_gather x1, waiting for transfers between devices, local(): lax.all_gather(keys_own, 'ctx', axis=0, tiled=True)  47.1 us
    all_gather x1, waiting for transfers between devices, local(): piece_query = lax.all_gather(queries, 'ctx', axis=0, tiled=True)  40.8 us
    all_to_all x1, waiting for transfers between devices, local(): lax.all_to_all(outgoing.astype(jnp.bfloat16), 'table', split_axis=0, conc...  32.2 us
    all_to_all x1, blocking collectives, local(): lax.all_to_all(requests, 'table', split_axis=0, concat_axis=0, tiled=True)  28.3 us
  transfers between devices with their start and end apart: 7, of which 7 were waited for; matrix products, arithmetic and copies ran while one was open for 7% of the time, Pallas kernels for 0%

commit v1 on v0

v1 whole, which is shorter than its diff:
```python
import jax
import jax.numpy as jnp
from jax import lax
from jax.experimental import pallas as pl
from jax.experimental.pallas import tpu as pltpu
from jax.sharding import PartitionSpec as P

EPSILON = 1e-05
BLOCK = 128
WIDTH = 512
HEADS = 4
HEAD_DIM = 128
TABLES = 32
GROUPS = 16
SHARD_ROWS = 512
QUERIES = BLOCK // HEADS
SEQ = BLOCK * GROUPS
SPAN = 4 * BLOCK
SCALE = HEAD_DIM ** (-0.5)
PIECE = 2 * BLOCK + 2 * QUERIES
MAIN = 8
SENT = TABLES * MAIN
PACKED = WIDTH + WIDTH // 2

F32 = jnp.float32
BF16 = jnp.bfloat16


def dot(a, b):
    return jnp.dot(a, b, preferred_element_type=F32)


def dot_nt(a, b):
    return lax.dot_general(a, b, (((1,), (1,)), ((), ())), preferred_element_type=F32)


def dot_tn(a, b):
    return lax.dot_general(a, b, (((0,), (0,)), ((), ())), preferred_element_type=F32)


def iota(shape, dim):
    return lax.broadcasted_iota(jnp.int32, shape, dim)


def one_hot(mask):
    return jnp.where(mask, 1.0, 0.0).astype(BF16)


def normalize(values):
    centre = values - jnp.mean(values, axis=-1, keepdims=True)
    scale_inv = lax.rsqrt(jnp.mean(centre * centre, axis=-1, keepdims=True) + EPSILON)
    return (centre * scale_inv, scale_inv)


def norm_back(grad, normed, scale_inv):
    return scale_inv * (
        grad
        - jnp.mean(grad, axis=-1, keepdims=True)
        - normed * jnp.mean(grad * normed, axis=-1, keepdims=True)
    )


def index_kernel(length_ref, ids_ref, slot_ref, send_ref, info_ref):
    ids = ids_ref[...]
    event = iota((1, BLOCK), 1)
    valid = lax.axis_index("ctx") * BLOCK + event < length_ref[0]
    row = iota((BLOCK, BLOCK), 0)
    table = slot_ref[...]
    rows_hot = one_hot(row == (ids >> 7))
    high = dot_tn((table >> 7).astype(F32).astype(BF16), rows_hot)
    low = dot_tn((table & 127).astype(F32).astype(BF16), rows_hot)
    both = jnp.where(row == (ids & 127), high * 128.0 + low, 0.0)
    slots = jnp.sum(both, axis=0, keepdims=True).astype(jnp.int32)
    owner = jnp.where(valid, slots >> 9, TABLES)
    wanted = (slots & (SHARD_ROWS - 1)) + 1
    owned = iota((TABLES, BLOCK), 0) == owner
    earlier = dot(one_hot(owned), one_hot(row < iota((BLOCK, BLOCK), 1)))
    rank = jnp.sum(jnp.where(owned, earlier, 0.0), axis=0, keepdims=True).astype(jnp.int32)
    head = jnp.where(valid & (rank < MAIN), owner * MAIN + rank, -1000)
    tail = jnp.where(valid & (rank >= MAIN), owner * MAIN + rank - MAIN, -1000)
    info_ref[...] = jnp.concatenate([head, tail, head, tail, head, tail, head, tail], axis=0)
    place = iota((SENT, BLOCK), 0)
    in_head = one_hot(place == head)
    in_tail = one_hot((place == tail) | (place == tail + 4))
    wide = jnp.broadcast_to(wanted, (BLOCK, BLOCK))
    wide_high = (wide >> 5).astype(F32).astype(BF16)
    wide_low = (wide & 31).astype(F32).astype(BF16)
    ask_head = dot_nt(in_head, wide_high) * 32.0 + dot_nt(in_head, wide_low)
    ask_tail = dot_nt(in_tail, wide_high) * 32.0 + dot_nt(in_tail, wide_low)
    asked = jnp.where(iota((SENT, BLOCK), 1) < BLOCK // 2, ask_head, ask_tail)
    send_ref[...] = asked.astype(jnp.int32)


def spread(asked):
    turned = pltpu.roll(asked, BLOCK // 2, 1)
    left = iota((SENT, BLOCK), 1) < BLOCK // 2
    return jnp.where(left, asked, turned), jnp.where(left, turned, asked)


def gather_kernel(asked_ref, slab_ref, out_ref):
    head, tail = spread(asked_ref[...])
    column = iota((SENT, BLOCK), 1) + 1
    spans = [column + BLOCK * k for k in range(SHARD_ROWS // BLOCK)]
    slab = slab_ref[...].astype(BF16)
    hot_head = jnp.concatenate([one_hot(head == span) for span in spans], axis=1)
    hot_tail = jnp.concatenate([one_hot(tail == span) for span in spans], axis=1)
    out_ref[:, :WIDTH] = dot(hot_head, slab).astype(BF16)
    rest = dot(hot_tail, slab)
    half = WIDTH // 2
    first = (iota((SENT, half), 0) & 7) < 4
    out_ref[:, WIDTH:] = jnp.where(first, rest[:, :half], rest[:, half:]).astype(BF16)


def cotangent_kernel(length_ref, upstream_ref, proj_out_ref, d_gated_ref):
    place = lax.axis_index("ctx") * BLOCK + iota((BLOCK, WIDTH), 0)
    d_out = jnp.where(place < length_ref[0], upstream_ref[...], jnp.zeros((), BF16))
    d_gated_ref[...] = dot_nt(d_out, proj_out_ref[...])


def place_masks(info_ref):
    place = iota((SENT, BLOCK), 0)
    head, tail = info_ref[0:1, :], info_ref[1:2, :]
    return one_hot(place == head), one_hot(place == tail), one_hot(place == tail + 4)


def project_kernel(
    info_ref, rows_ref, proj_in_ref, d_gated_ref, send_ref, embedded_ref, gate_ref, slope_ref
):
    in_head, in_first, in_second = place_masks(info_ref)
    half = WIDTH // 2
    rest = rows_ref[:, WIDTH:]
    embedded = dot_tn(in_head, rows_ref[:, :WIDTH]) + jnp.concatenate(
        [dot_tn(in_first, rest), dot_tn(in_second, rest)], axis=1
    )
    embedded_ref[...] = embedded.astype(BF16)
    normed = normalize(embedded)[0].astype(BF16)

    def part(k):
        return dot(normed, proj_in_ref[:, k * WIDTH : (k + 1) * WIDTH])

    def silu(values):
        sig = jax.nn.sigmoid(values)
        return values * sig, sig * (1.0 + values * (1.0 - sig))

    gate, slope_gate = silu(part(0))
    value, slope_value = silu(part(1))
    slope_ref[:, :WIDTH] = slope_gate
    slope_ref[:, WIDTH:] = slope_value
    gate = gate.astype(BF16)
    gate_ref[...] = gate
    value = value.astype(BF16)
    query = part(2).astype(BF16)
    key = part(3).astype(BF16)
    d_hat = (d_gated_ref[...] * gate.astype(F32)).astype(BF16)
    for h in range(HEADS):
        cols = slice(h * HEAD_DIM, (h + 1) * HEAD_DIM)
        for g in range(HEADS):
            rows = slice(g * QUERIES, (g + 1) * QUERIES)
            chunk = HEADS * g + h
            send_ref[chunk, 0:BLOCK, :] = key[:, cols]
            send_ref[chunk, BLOCK : 2 * BLOCK, :] = value[:, cols]
            send_ref[chunk, 2 * BLOCK : 2 * BLOCK + QUERIES, :] = query[rows, cols]
            send_ref[chunk, 2 * BLOCK + QUERIES :, :] = d_hat[rows, cols]


def allowed_mask():
    group = lax.axis_index("ctx") // HEADS
    lane = iota((SPAN, BLOCK), 1)
    place = (lane // QUERIES) * BLOCK + group * QUERIES + lane % QUERIES
    return iota((SPAN, BLOCK), 0) <= place


def span_keys(recv_ref, j):
    chunks = slice(4 * j, 4 * j + 4)
    key = recv_ref[chunks, 0:BLOCK, :].reshape(SPAN, HEAD_DIM)
    value = recv_ref[chunks, BLOCK : 2 * BLOCK, :].reshape(SPAN, HEAD_DIM)
    return key, value


def attend_kernel(recv_ref, att_ref, d_hat_ref, stats_ref):
    query = recv_ref[:, 2 * BLOCK : 2 * BLOCK + QUERIES, :].reshape(SPAN, HEAD_DIM)
    mask = allowed_mask()
    for j in range(4):
        key, value = span_keys(recv_ref, j)
        start = j * BLOCK
        half = dot_nt(key, query[start:, :]) * (0.5 * SCALE)
        weight = half + half * jnp.tanh(half)
        weight = jnp.concatenate(
            [jnp.where(mask, weight[:, :BLOCK], 0.0), weight[:, BLOCK:]], axis=1
        ) if j < 3 else jnp.where(mask, weight, 0.0)
        part = dot_tn(value, weight.astype(BF16))
        if j == 0:
            att_ref[...] = part
        else:
            att_ref[:, start:] += part
    d_hat = recv_ref[:, 2 * BLOCK + QUERIES :, :].reshape(SPAN, HEAD_DIM)
    d_hat = d_hat.astype(F32).T
    d_hat_ref[...] = d_hat
    att = att_ref[...]
    mean = jnp.mean(att, axis=0, keepdims=True)
    centre = att - mean
    d_mean = jnp.mean(d_hat, axis=0, keepdims=True)
    spread_sum = jnp.sum(centre * centre, axis=0, keepdims=True)
    cross_sum = jnp.sum(centre * (d_hat - d_mean), axis=0, keepdims=True)
    rows = jnp.concatenate(
        [mean, spread_sum, d_mean, cross_sum, mean, spread_sum, d_mean, cross_sum], axis=0
    )
    for k in range(HEADS):
        stats_ref[k] = rows


def backward_kernel(recv_ref, att_ref, d_hat_ref, stats_ref, send_ref, d_query_ref):
    query = recv_ref[:, 2 * BLOCK : 2 * BLOCK + QUERIES, :].reshape(SPAN, HEAD_DIM)
    mask = allowed_mask()
    stats = [stats_ref[k] for k in range(HEADS)]

    def average(row):
        return sum(s[row : row + 1, :] for s in stats) / HEADS

    mean, d_mean = average(0), average(2)
    spread_mean = average(1) / HEAD_DIM + sum(
        (s[0:1, :] - mean) * (s[0:1, :] - mean) for s in stats
    ) / HEADS
    cross_mean = average(3) / HEAD_DIM + sum(
        (s[0:1, :] - mean) * (s[2:3, :] - d_mean) for s in stats
    ) / HEADS
    inv = lax.rsqrt(spread_mean + EPSILON)
    att = att_ref[...]
    att_hat = (att - mean) * inv
    d_att = (inv * (d_hat_ref[...] - d_mean - att_hat * (inv * cross_mean))).astype(BF16)
    out_att = att.T.astype(BF16)
    for j in range(4):
        key, value = span_keys(recv_ref, j)
        start = j * BLOCK
        half = dot_nt(key, query[start:, :]) * (0.5 * SCALE)
        th = jnp.tanh(half)
        weight = half + half * th
        slope = (0.5 * SCALE) * ((1.0 + th) + weight * (1.0 - th))
        d_score = dot(value, d_att[:, start:]) * slope

        def masked(values):
            first = jnp.where(mask, values[:, :BLOCK], 0.0)
            if j == 3:
                return first.astype(BF16)
            return jnp.concatenate([first, values[:, BLOCK:]], axis=1).astype(BF16)

        weight, d_score = masked(weight), masked(d_score)
        d_key = dot(d_score, query[start:, :]).astype(BF16)
        d_value = dot_nt(weight, d_att[:, start:]).astype(BF16)
        part = dot_tn(key, d_score)
        if j == 0:
            d_query_ref[...] = part
        else:
            d_query_ref[:, start:] += part
        for k in range(4):
            rows = slice(k * BLOCK, (k + 1) * BLOCK)
            send_ref[4 * j + k, 0:BLOCK, :] = d_key[rows]
            send_ref[4 * j + k, BLOCK : 2 * BLOCK, :] = d_value[rows]
    d_query = d_query_ref[...].T.astype(BF16)
    for c in range(GROUPS):
        rows = slice(c * QUERIES, (c + 1) * QUERIES)
        send_ref[c, 2 * BLOCK : 2 * BLOCK + QUERIES, :] = d_query[rows]
        send_ref[c, 2 * BLOCK + QUERIES :, :] = out_att[rows]


def collect(recv_ref, first, rows):
    return jnp.concatenate(
        [
            jnp.concatenate([recv_ref[HEADS * g + h, first : first + rows, :] for g in range(HEADS)], axis=0)
            for h in range(HEADS)
        ],
        axis=1,
    ).astype(F32)


def collect_sum(recv_ref, first):
    def head(h):
        return sum(
            recv_ref[HEADS * g + h, first : first + BLOCK, :].astype(F32) for g in range(HEADS)
        )

    return jnp.concatenate([head(h) for h in range(HEADS)], axis=1)


def finish_kernel(
    length_ref,
    info_ref,
    recv_ref,
    embedded_ref,
    slope_ref,
    d_gated_ref,
    upstream_ref,
    proj_in_ref,
    out_ref,
    att_hat_ref,
):
    att_hat = normalize(collect(recv_ref, 2 * BLOCK + QUERIES, QUERIES))[0]
    att_hat_ref[...] = att_hat
    d_value = collect_sum(recv_ref, BLOCK) * slope_ref[:, WIDTH:]
    d_gate = d_gated_ref[...] * att_hat * slope_ref[:, :WIDTH]
    d_query = collect(recv_ref, 2 * BLOCK, QUERIES)
    d_key = collect_sum(recv_ref, 0)
    d_normed = jnp.zeros((BLOCK, WIDTH), F32)
    for k, part in enumerate((d_gate, d_value, d_query, d_key)):
        d_normed += dot_nt(part.astype(BF16), proj_in_ref[:, k * WIDTH : (k + 1) * WIDTH])
    normed, inv_std = normalize(embedded_ref[...].astype(F32))
    place = lax.axis_index("ctx") * BLOCK + iota((BLOCK, WIDTH), 0)
    d_embedded = jnp.where(
        place < length_ref[0],
        upstream_ref[...].astype(F32) + norm_back(d_normed, normed, inv_std),
        0.0,
    ).astype(BF16)
    in_head, in_first, in_second = place_masks(info_ref)
    half = WIDTH // 2
    out_ref[:, :WIDTH] = dot(in_head, d_embedded).astype(BF16)
    out_ref[:, WIDTH:] = (
        dot(in_first, d_embedded[:, :half]) + dot(in_second, d_embedded[:, half:])
    ).astype(BF16)


def output_kernel(length_ref, att_hat_ref, gate_ref, embedded_ref, proj_out_ref, out_ref):
    gated = (att_hat_ref[...] * gate_ref[...].astype(F32)).astype(BF16)
    total = embedded_ref[...].astype(F32) + dot(gated, proj_out_ref[...])
    place = lax.axis_index("ctx") * BLOCK + iota((BLOCK, WIDTH), 0)
    out_ref[...] = jnp.where(place < length_ref[0], total, 0.0).astype(BF16)


def scatter_kernel(asked_ref, arrived_ref, out_ref):
    head, tail = spread(asked_ref[...])
    head_across = head.astype(F32).T
    tail_across = tail.astype(F32).T
    half = WIDTH // 2
    first = (iota((BLOCK, SENT), 1) & 7) < 4
    rows = (iota((BLOCK, SENT), 0) + 1).astype(F32)
    main = arrived_ref[:, :WIDTH]
    rest = arrived_ref[:, WIDTH:]
    for k in range(SHARD_ROWS // BLOCK):
        here = rows + float(BLOCK * k)
        hot_head = one_hot(head_across == here)
        in_tail = tail_across == here
        total = dot(hot_head, main)
        out = slice(k * BLOCK, (k + 1) * BLOCK)
        out_ref[out, :half] = (total[:, :half] + dot(one_hot(in_tail & first), rest)).astype(BF16)
        out_ref[out, half:] = (
            total[:, half:] + dot(one_hot(in_tail & jnp.logical_not(first)), rest)
        ).astype(BF16)


def sum_kernel(parts_ref, out_ref):
    total = parts_ref[0].astype(F32)
    for k in range(1, GROUPS):
        total += parts_ref[k].astype(F32)
    out_ref[...] = total


SCALAR = pl.BlockSpec(memory_space=pltpu.SMEM)
WHOLE = pl.BlockSpec(memory_space=pltpu.VMEM)


def run(kernel, name, outs, *args, scalars=0, scratch=()):
    single = not isinstance(outs, (list, tuple))
    return pl.pallas_call(
        kernel,
        out_shape=outs,
        in_specs=[SCALAR] * scalars + [WHOLE] * (len(args) - scalars),
        out_specs=WHOLE if single else [WHOLE] * len(outs),
        scratch_shapes=scratch,
        compiler_params=pltpu.CompilerParams(vmem_limit_bytes=40 * 1024 * 1024),
        name=name,
    )(*args)


def shape(*dims, dtype=BF16):
    return jax.ShapeDtypeStruct(dims, dtype)


def swap(array, axis, groups=None):
    return lax.all_to_all(
        array, axis, split_axis=0, concat_axis=0, tiled=True, axis_index_groups=groups
    )


def local(item_ids, history_len, item_slot, table_slab, proj_in, proj_out, upstream):
    upstream = upstream[0]
    requests, info = run(
        index_kernel,
        "index",
        [shape(SENT, BLOCK, dtype=jnp.int32), shape(8, BLOCK, dtype=jnp.int32)],
        history_len,
        item_ids,
        item_slot.reshape(BLOCK, BLOCK),
        scalars=1,
    )
    asked = swap(requests.reshape(TABLES, MAIN, BLOCK), "table").reshape(SENT, BLOCK)
    d_gated = run(
        cotangent_kernel,
        "cotangent",
        shape(BLOCK, WIDTH, dtype=F32),
        history_len,
        upstream,
        proj_out,
        scalars=1,
    )
    rows_out = run(gather_kernel, "gather", shape(SENT, PACKED), asked, table_slab)
    rows = swap(rows_out.reshape(TABLES, MAIN, PACKED), "table").reshape(SENT, PACKED)
    send, embedded, gate, slope = run(
        project_kernel,
        "project",
        [
            shape(GROUPS, PIECE, HEAD_DIM),
            shape(BLOCK, WIDTH),
            shape(BLOCK, WIDTH),
            shape(BLOCK, 2 * WIDTH, dtype=F32),
        ],
        info,
        rows,
        proj_in,
        d_gated,
    )
    recv = swap(send, "ctx")
    att, d_hat, stats = run(
        attend_kernel,
        "attend",
        [
            shape(HEAD_DIM, SPAN, dtype=F32),
            shape(HEAD_DIM, SPAN, dtype=F32),
            shape(HEADS, 8, SPAN, dtype=F32),
        ],
        recv,
    )
    lines = [[HEADS * g + h for h in range(HEADS)] for g in range(GROUPS // HEADS)]
    stats = swap(stats, "ctx", lines)
    send_back = run(
        backward_kernel,
        "backward",
        shape(GROUPS, PIECE, HEAD_DIM),
        recv,
        att,
        d_hat,
        stats,
        scratch=[pltpu.VMEM((HEAD_DIM, SPAN), F32)],
    )
    back = swap(send_back, "ctx")
    outgoing, att_hat = run(
        finish_kernel,
        "finish",
        [shape(SENT, PACKED), shape(BLOCK, WIDTH, dtype=F32)],
        history_len,
        info,
        back,
        embedded,
        slope,
        d_gated,
        upstream,
        proj_in,
        scalars=1,
    )
    arrived = swap(outgoing.reshape(TABLES, MAIN, PACKED), "table").reshape(SENT, PACKED)
    layer_out = run(
        output_kernel,
        "output",
        shape(BLOCK, WIDTH),
        history_len,
        att_hat,
        gate,
        embedded,
        proj_out,
        scalars=1,
    )
    sums = run(scatter_kernel, "scatter", shape(SHARD_ROWS, WIDTH), asked, arrived)
    parts = swap(sums.reshape(GROUPS, SHARD_ROWS // GROUPS, WIDTH), "ctx")
    table_grad = run(
        sum_kernel, "total", shape(SHARD_ROWS // GROUPS, WIDTH, dtype=F32), parts
    )
    return (layer_out[None], table_grad)


def solution(mesh):
    placed = (
        P("table", "ctx"),
        P("table"),
        P(),
        P("table", None),
        P(),
        P(),
        P("table", "ctx", None),
    )
    return jax.shard_map(
        local,
        mesh=mesh,
        in_specs=placed,
        out_specs=(P("table", "ctx", None), P(("table", "ctx"), None)),
        check_vma=False,
    )
```

time: 524 us -> 184 us (0.35)
  waiting for transfers between devices: 366 us -> 36.7 us
  blocking collectives: 28.3 us -> 121 us
  matrix products: 40 us -> 0 us
  local copies, waits for them, and re-layouts: 29 us -> 4.29 us
  other arithmetic: 24.6 us -> 0 us
  between operations: 15.4 us -> 1.4 us
  Pallas kernels: 0 us -> 11.2 us
  starting transfers between devices: 19.4 us -> 8.71 us
    all_gather x4 -> x0, waiting for transfers between devices: 205 us -> none  [the longest x1 62.6 us: local(): piece_grad = lax.all_gather(d_attn, 'ctx', axis=0, tiled=True)]
    all_to_all x1 -> x5, blocking collectives: 28.3 us -> 121 us  [swap(): lax.all_to_all(array, axis, split_axis=0, concat_axis=0, tiled=True, axis...]
    reduce_scatter x1 -> x0, waiting for transfers between devices: 73.2 us -> none  [local(): lax.psum_scatter(shard_sums.astype(jnp.bfloat16), 'ctx', scatter_dimensio...]
    all_to_all x2, waiting for transfers between devices: 86.7 us -> 36.7 us  [swap(): lax.all_to_all(array, axis, split_axis=0, concat_axis=0, tiled=True, axis...]
    dot_general x10 -> x0, matrix products: 40 us -> none  [the longest x1 7.12 us: local(): jnp.einsum('hqk,khd->qhd', d_scores, key_heads, preferred_element_type=jn...]
    pallas_call x0 -> x10, Pallas kernels: none -> 11.2 us  [run(): pl.pallas_call(kernel, out_shape=outs, in_specs=[SCALAR] * scalars + [WHO...]
    all_to_all x2, starting transfers between devices: 19.2 us -> 8.71 us  [swap(): lax.all_to_all(array, axis, split_axis=0, concat_axis=0, tiled=True, axis...]
    reshape x5 -> x0, local copies, waits for them, and re-layouts: 9.66 us -> none  [the longest x1 3.95 us: local(): key_heads = all_keys.reshape(seq_len, head_count, HEAD_DIM)]
  transfers between devices with their start and end apart: 7 -> 2, of which waited for: 7 -> 2; matrix products, arithmetic and copies ran while one was open for 7% -> 0% of each run, Pallas kernels for 0% -> 1%
where the time goes in v1:
time: 184 us; the launch traced here: 183 us
  blocking collectives  121 us (66%)
  waiting for transfers between devices  36.7 us (20%)
  Pallas kernels  11.2 us (6%)
  starting transfers between devices  8.71 us (5%)
  local copies, waits for them, and re-layouts  4.29 us (2%)
    all_to_all x5, blocking collectives, swap(): lax.all_to_all(array, axis, split_axis=0, concat_axis=0, tiled=True, axis...  121 us
    all_to_all x2, waiting for transfers between devices, swap(): lax.all_to_all(array, axis, split_axis=0, concat_axis=0, tiled=True, axis...  36.7 us
    pallas_call x10, Pallas kernels, run(): pl.pallas_call(kernel, out_shape=outs, in_specs=[SCALAR] * scalars + [WHO...  11.2 us
    all_to_all x2, starting transfers between devices, swap(): lax.all_to_all(array, axis, split_axis=0, concat_axis=0, tiled=True, axis...  8.71 us
    unnamed x18, local copies, waits for them, and re-layouts  4.29 us
  transfers between devices with their start and end apart: 2, of which 2 were waited for; matrix products, arithmetic and copies ran while one was open for 0% of the time, Pallas kernels for 1%

profile of v1, /device:TPU:1, one launch (start us, length us, event | category | flops | bytes accessed | tf_op | source)
XLA Modules:
  0.0 183.2 jit_solution(6378110985697071924)
XLA Ops:
  1.3 0.8 copy-done.7
  2.1 0.7 copy-done.8
  2.8 0.6 index.1
  3.4 32.5 %all_to_all.35 = s32[32,8,128]{2,1,0:T(8,128)S(1)} all-to-all(s32[32,8,128]{2,1,0:T(8,128)S(1)} %bitcast.17), channel_id=1, replica_groups=mesh['table'=32,'ctx'=16] {'table'}, dimensions={0} | all-to-all | bytes 262144 | tf_op jit(solution)/shard_map/all_to_all | solution.py:378
  35.9 1.2 copy-done.2
  37.1 1.3 gather.1
  38.4 5.1 %all-to-all-start.1 = ((bf16[32,8,768]{2,1,0:T(8,128)(2,1)}), bf16[32,8,768]{2,1,0:T(8,128)(2,1)S(1)}, u32[]{:S(2)}, u32[]{:S(2)}) async-start(bf16[32,8,768]{2,1,0:T(8,128)(2,1)} %bitcast.3), calls=%async_computation.1 | async-start | bytes 786432 | tf_op jit(solution)/shard_map/all_to_all | solution.py:378
  43.5 0.9 copy-done.3
  44.4 0.3 cotangent.1.d_gated_ref
  44.7 26.8 %all-to-all-done.1 = bf16[32,8,768]{2,1,0:T(8,128)(2,1)S(1)} async-done(((bf16[32,8,768]{2,1,0:T(8,128)(2,1)}), bf16[32,8,768]{2,1,0:T(8,128)(2,1)S(1)}, u32[]{:S(2)}, u32[]{:S(2)}) %all-to-all-start.1) | async-done | bytes 393248 | tf_op jit(solution)/shard_map/all_to_all | solution.py:378
  71.6 0.9 project.1
  72.5 0.6 copy-done.5
  73.1 25.7 %all_to_all.36.recv_ref = bf16[16,320,128]{2,1,0:T(8,128)(2,1)S(1)} all-to-all(bf16[16,320,128]{2,1,0:T(8,128)(2,1)S(1)} %get-tuple-element.15), channel_id=1, replica_groups=mesh['table'=32,'ctx'=16] {'ctx'}, dimensions={0} | all-to-all | bytes 2621440 | tf_op jit(solution)/shard_map/all_to_all | solution.py:378
  98.9 1.4 attend.1
  100.3 6.8 %all_to_all.37.stats_ref = f32[4,8,512]{2,1,0:T(8,128)S(1)} all-to-all(f32[4,8,512]{2,1,0:T(8,128)S(1)} %get-tuple-element.18), channel_id=1, replica_groups={{0,1,2,3},{4,5,6,7},{8,9,10,11},{12,13,14,15},{16,17,18,19},{20,21,22,2..., dimensions={0} | all-to-all | bytes 131072 | tf_op jit(solution)/shard_map/all_to_all | solution.py:378
  107.1 2.4 %backward.1 = bf16[16,320,128]{2,1,0:T(8,128)(2,1)S(1)} custom-call(bf16[16,320,128]{2,1,0:T(8,128)(2,1)S(1)} %all_to_all.36.recv_ref, f32[128,512]{1,0:T(8,128)S(1)} %get-tuple-element.16.att_ref, f32[128,512]{1,0:T(8,128)S(1)} %get-tuple-element.17.d_hat_ref, f32[4,8,512]{2,1,0:T(8,128)S(1)} %all_to_all.37.stats_ref), custom_call_target="tpu_custom_call" | custom-call | tf_op jit(solution)/shard_map/backward/pallas_call | solution.py:362
  109.6 20.1 %all_to_all.38.recv_ref = bf16[16,320,128]{2,1,0:T(8,128)(2,1)S(1)} all-to-all(bf16[16,320,128]{2,1,0:T(8,128)(2,1)S(1)} %backward.1), channel_id=1, replica_groups=mesh['table'=32,'ctx'=16] {'ctx'}, dimensions={0} | all-to-all | bytes 2621440 | tf_op jit(solution)/shard_map/all_to_all | solution.py:378
  129.7 1.3 finish.1
  131.0 35.7 %all_to_all.39 = bf16[32,8,768]{2,1,0:T(8,128)(2,1)S(1)} all-to-all(bf16[32,8,768]{2,1,0:T(8,128)(2,1)S(1)} %bitcast.16), channel_id=1, replica_groups=mesh['table'=32,'ctx'=16] {'table'}, dimensions={0} | all-to-all | bytes 786432 | tf_op jit(solution)/shard_map/all_to_all | solution.py:378
  166.7 1.4 scatter.1
  168.1 3.6 %all-to-all-start.6 = ((bf16[16,32,512]{2,1,0:T(8,128)(2,1)}), bf16[16,32,512]{2,1,0:T(8,128)(2,1)S(1)}, u32[]{:S(2)}, u32[]{:S(2)}) async-start(bf16[16,32,512]{2,1,0:T(8,128)(2,1)} %bitcast.9), calls=%async_computation.6 | async-start | bytes 1048576 | tf_op jit(solution)/shard_map/all_to_all | solution.py:378
  171.7 0.9 output.1
  172.6 9.9 %all-to-all-done.6.parts_ref = bf16[16,32,512]{2,1,0:T(8,128)(2,1)S(1)} async-done(((bf16[16,32,512]{2,1,0:T(8,128)(2,1)}), bf16[16,32,512]{2,1,0:T(8,128)(2,1)S(1)}, u32[]{:S(2)}, u32[]{:S(2)}) %all-to-all-start.6) | async-done | bytes 524320 | tf_op jit(solution)/shard_map/all_to_all | solution.py:378
  182.5 0.7 total.1
  (13 shorter events, 0.0 us)
Async XLA Ops:
  1.3 0.8 copy-start.7
  2.1 0.7 copy-start.8
  3.3 40.2 %copy-start.1 = (bf16[512,512]{1,0:T(8,128)(2,1)S(1)}, bf16[512,512]{1,0:T(8,128)(2,1)}, u32[]{:S(2)}) copy-start(bf16[512,512]{1,0:T(8,128)(2,1)} %proj_out_ref.3) | copy-start | bytes 1572868
  35.9 1.2 copy-start.2
  37.1 34.4 %copy-start = (bf16[512,2048]{1,0:T(8,128)(2,1)S(1)}, bf16[512,2048]{1,0:T(8,128)(2,1)}, u32[]{:S(2)}) copy-start(bf16[512,2048]{1,0:T(8,128)(2,1)} %proj_in_ref.3) | copy-start | bytes 6291460
  38.4 33.2 %all-to-all-start.1 = ((bf16[32,8,768]{2,1,0:T(8,128)(2,1)}), bf16[32,8,768]{2,1,0:T(8,128)(2,1)S(1)}, u32[]{:S(2)}, u32[]{:S(2)}) async-start(bf16[32,8,768]{2,1,0:T(8,128)(2,1)} %bitcast.3), calls=%async_computation.1 | async-start | bytes 786432 | tf_op jit(solution)/shard_map/all_to_all | solution.py:378
  43.5 0.9 copy-start.3
  72.5 0.7 copy-start.5
  109.6 20.1 %copy-start.4 = (bf16[1,128,512]{2,1,0:T(8,128)(2,1)S(1)}, bf16[1,128,512]{2,1,0:T(8,128)(2,1)}, u32[]{:S(2)}) copy-start(bf16[1,128,512]{2,1,0:T(8,128)(2,1)} %param.13) | copy-start | bytes 393220
  131.0 40.7 %copy-start.6 = (bf16[128,512]{1,0:T(8,128)(2,1)S(1)}, bf16[128,512]{1,0:T(8,128)(2,1)}, u32[]{:S(2)}) copy-start(bf16[128,512]{1,0:T(8,128)(2,1)} %copy-done.5) | copy-start | bytes 393220
  168.1 14.4 %all-to-all-start.6 = ((bf16[16,32,512]{2,1,0:T(8,128)(2,1)}), bf16[16,32,512]{2,1,0:T(8,128)(2,1)S(1)}, u32[]{:S(2)}, u32[]{:S(2)}) async-start(bf16[16,32,512]{2,1,0:T(8,128)(2,1)} %bitcast.9), calls=%async_computation.6 | async-start | bytes 1048576 | tf_op jit(solution)/shard_map/all_to_all | solution.py:378

commit v2 on v1

--- a/solution.py
+++ b/solution.py
@@ -52,6 +52,13 @@
     return (centre * scale_inv, scale_inv)
 
 
+def silu_and_slope(values):
+    half = 0.5 * values
+    th = jnp.tanh(half)
+    out = half + half * th
+    return out, 0.5 * ((1.0 + th) + out * (1.0 - th))
+
+
 def norm_back(grad, normed, scale_inv):
     return scale_inv * (
         grad
@@ -63,7 +70,8 @@
 def index_kernel(length_ref, ids_ref, slot_ref, send_ref, info_ref):
     ids = ids_ref[...]
     event = iota((1, BLOCK), 1)
-    valid = lax.axis_index("ctx") * BLOCK + event < length_ref[0]
+    length = length_ref[...]
+    valid = lax.axis_index("ctx") * BLOCK + event < length
     row = iota((BLOCK, BLOCK), 0)
     table = slot_ref[...]
     rows_hot = one_hot(row == (ids >> 7))
@@ -74,84 +82,98 @@
     owner = jnp.where(valid, slots >> 9, TABLES)
     wanted = (slots & (SHARD_ROWS - 1)) + 1
     owned = iota((TABLES, BLOCK), 0) == owner
-    earlier = dot(one_hot(owned), one_hot(row < iota((BLOCK, BLOCK), 1)))
+    owned_hot = one_hot(owned)
+    earlier = dot(owned_hot, one_hot(row < iota((BLOCK, BLOCK), 1)))
     rank = jnp.sum(jnp.where(owned, earlier, 0.0), axis=0, keepdims=True).astype(jnp.int32)
     head = jnp.where(valid & (rank < MAIN), owner * MAIN + rank, -1000)
     tail = jnp.where(valid & (rank >= MAIN), owner * MAIN + rank - MAIN, -1000)
-    info_ref[...] = jnp.concatenate([head, tail, head, tail, head, tail, head, tail], axis=0)
+    lengths = jnp.broadcast_to(length, (6, BLOCK))
+    info_ref[...] = jnp.concatenate([head, tail, lengths], axis=0)
+    ranked = jnp.where(row < BLOCK // 2, row & 7, MAIN + (row & 3)) == rank
+    wanted_high = jnp.where(ranked, (wanted >> 5).astype(F32), 0.0).astype(BF16)
+    wanted_low = jnp.where(ranked, (wanted & 31).astype(F32), 0.0).astype(BF16)
+    asked = dot_nt(owned_hot, wanted_high) * 32.0 + dot_nt(owned_hot, wanted_low)
+    send_ref[...] = asked.astype(jnp.int32)
+
+
+def asked_rows(asked_ref):
+    asked = asked_ref[...].reshape(TABLES, BLOCK).astype(F32)
+    turned = pltpu.roll(asked, BLOCK // 2, 1)
+    left = iota((TABLES, BLOCK), 1) < BLOCK // 2
+    both = []
+    for wanted in (jnp.where(left, asked, turned), jnp.where(left, turned, asked)):
+        parts = []
+        for k in range(SENT // BLOCK):
+            own = iota((TABLES, BLOCK), 0) == (iota((TABLES, BLOCK), 1) >> 3) + k * BLOCK // MAIN
+            parts.append(jnp.sum(jnp.where(own, wanted, 0.0), axis=0, keepdims=True))
+        both.append(jnp.concatenate(parts, axis=1))
+    return both
+
+
+def gather_kernel(asked_ref, slab_ref, out_ref, rows_ref):
+    head, tail = asked_rows(asked_ref)
+    first = (iota((1, SENT), 1) & 7) < 4
+    tail_first = jnp.where(first, tail, 0.0)
+    tail_second = jnp.where(first, 0.0, tail)
+    rows_ref[...] = jnp.concatenate(
+        [head, tail_first, tail_second, head, tail_first, tail_second, head, tail], axis=0
+    )
+    half = WIDTH // 2
+    row = (iota((SHARD_ROWS, SENT), 0) + 1).astype(F32)
+    out_ref[:, :WIDTH] = dot_tn(one_hot(row == head), slab_ref[...]).astype(BF16)
+    rest = dot_tn(one_hot(row == tail_first), slab_ref[:, :half])
+    rest += dot_tn(one_hot(row == tail_second), slab_ref[:, half:])
+    out_ref[:, WIDTH:] = rest.astype(BF16)
+
+
+def valid_rows(d_gated_ref):
+    length = d_gated_ref[BLOCK + 2 : BLOCK + 3, 0:1].astype(jnp.int32)
+    return lax.axis_index("ctx") * BLOCK + iota((BLOCK, WIDTH), 0) < length
+
+
+def place_masks(d_gated_ref):
     place = iota((SENT, BLOCK), 0)
-    in_head = one_hot(place == head)
-    in_tail = one_hot((place == tail) | (place == tail + 4))
-    wide = jnp.broadcast_to(wanted, (BLOCK, BLOCK))
-    wide_high = (wide >> 5).astype(F32).astype(BF16)
-    wide_low = (wide & 31).astype(F32).astype(BF16)
-    ask_head = dot_nt(in_head, wide_high) * 32.0 + dot_nt(in_head, wide_low)
-    ask_tail = dot_nt(in_tail, wide_high) * 32.0 + dot_nt(in_tail, wide_low)
-    asked = jnp.where(iota((SENT, BLOCK), 1) < BLOCK // 2, ask_head, ask_tail)
-    send_ref[...] = asked.astype(jnp.int32)
-
-
-def spread(asked):
-    turned = pltpu.roll(asked, BLOCK // 2, 1)
-    left = iota((SENT, BLOCK), 1) < BLOCK // 2
-    return jnp.where(left, asked, turned), jnp.where(left, turned, asked)
-
-
-def gather_kernel(asked_ref, slab_ref, out_ref):
-    head, tail = spread(asked_ref[...])
-    column = iota((SENT, BLOCK), 1) + 1
-    spans = [column + BLOCK * k for k in range(SHARD_ROWS // BLOCK)]
-    slab = slab_ref[...].astype(BF16)
-    hot_head = jnp.concatenate([one_hot(head == span) for span in spans], axis=1)
-    hot_tail = jnp.concatenate([one_hot(tail == span) for span in spans], axis=1)
-    out_ref[:, :WIDTH] = dot(hot_head, slab).astype(BF16)
-    rest = dot(hot_tail, slab)
-    half = WIDTH // 2
-    first = (iota((SENT, half), 0) & 7) < 4
-    out_ref[:, WIDTH:] = jnp.where(first, rest[:, :half], rest[:, half:]).astype(BF16)
-
-
-def cotangent_kernel(length_ref, upstream_ref, proj_out_ref, d_gated_ref):
+    head = d_gated_ref[BLOCK : BLOCK + 1, :BLOCK].astype(jnp.int32)
+    tail = d_gated_ref[BLOCK + 1 : BLOCK + 2, :BLOCK].astype(jnp.int32)
+    return one_hot(place == head), one_hot(place == tail), one_hot(place == tail + 4)
+
+
+def prepare_kernel(slab_ref, info_ref, upstream_ref, proj_out_ref, narrow_ref, d_gated_ref):
+    narrow_ref[...] = slab_ref[...].astype(BF16)
     place = lax.axis_index("ctx") * BLOCK + iota((BLOCK, WIDTH), 0)
-    d_out = jnp.where(place < length_ref[0], upstream_ref[...], jnp.zeros((), BF16))
-    d_gated_ref[...] = dot_nt(d_out, proj_out_ref[...])
-
-
-def place_masks(info_ref):
-    place = iota((SENT, BLOCK), 0)
-    head, tail = info_ref[0:1, :], info_ref[1:2, :]
-    return one_hot(place == head), one_hot(place == tail), one_hot(place == tail + 4)
+    d_out = jnp.where(place < info_ref[2:3, 0:1], upstream_ref[...], jnp.zeros((), BF16))
+    d_gated_ref[:BLOCK, :] = dot_nt(d_out, proj_out_ref[...])
+    d_gated_ref[BLOCK:, :BLOCK] = info_ref[...].astype(F32)
+    d_gated_ref[BLOCK:, BLOCK:] = jnp.zeros((8, WIDTH - BLOCK), F32)
 
 
 def project_kernel(
-    info_ref, rows_ref, proj_in_ref, d_gated_ref, send_ref, embedded_ref, gate_ref, slope_ref
+    rows_ref, proj_in_ref, d_gated_ref, send_ref, embedded_ref, gate_ref, slope_ref
 ):
-    in_head, in_first, in_second = place_masks(info_ref)
+    in_head, in_first, in_second = place_masks(d_gated_ref)
     half = WIDTH // 2
     rest = rows_ref[:, WIDTH:]
     embedded = dot_tn(in_head, rows_ref[:, :WIDTH]) + jnp.concatenate(
         [dot_tn(in_first, rest), dot_tn(in_second, rest)], axis=1
     )
+    valid = valid_rows(d_gated_ref)
+    embedded = jnp.where(valid, embedded, 0.0)
     embedded_ref[...] = embedded.astype(BF16)
     normed = normalize(embedded)[0].astype(BF16)
 
     def part(k):
         return dot(normed, proj_in_ref[:, k * WIDTH : (k + 1) * WIDTH])
 
-    def silu(values):
-        sig = jax.nn.sigmoid(values)
-        return values * sig, sig * (1.0 + values * (1.0 - sig))
-
-    gate, slope_gate = silu(part(0))
-    value, slope_value = silu(part(1))
-    slope_ref[:, :WIDTH] = slope_gate
-    slope_ref[:, WIDTH:] = slope_value
-    gate = gate.astype(BF16)
+    gate_part = part(0)
+    value_part = part(1)
+    gate, slope_ref[:, :WIDTH] = silu_and_slope(gate_part)
+    value, slope_ref[:, WIDTH:] = silu_and_slope(value_part)
+    gate, value = gate.astype(BF16), value.astype(BF16)
     gate_ref[...] = gate
-    value = value.astype(BF16)
+    value = jnp.where(valid, value, jnp.zeros((), BF16))
     query = part(2).astype(BF16)
-    key = part(3).astype(BF16)
-    d_hat = (d_gated_ref[...] * gate.astype(F32)).astype(BF16)
+    key = jnp.where(valid, part(3), 0.0).astype(BF16)
+    d_hat = (d_gated_ref[:BLOCK, :] * gate.astype(F32)).astype(BF16)
     for h in range(HEADS):
         cols = slice(h * HEAD_DIM, (h + 1) * HEAD_DIM)
         for g in range(HEADS):
@@ -283,34 +305,30 @@
 
 
 def finish_kernel(
-    length_ref,
-    info_ref,
     recv_ref,
     embedded_ref,
+    gate_ref,
     slope_ref,
     d_gated_ref,
     upstream_ref,
     proj_in_ref,
     out_ref,
-    att_hat_ref,
+    gated_ref,
 ):
     att_hat = normalize(collect(recv_ref, 2 * BLOCK + QUERIES, QUERIES))[0]
-    att_hat_ref[...] = att_hat
+    valid = valid_rows(d_gated_ref)
+    gated_ref[...] = jnp.where(valid, att_hat * gate_ref[...].astype(F32), 0.0).astype(BF16)
     d_value = collect_sum(recv_ref, BLOCK) * slope_ref[:, WIDTH:]
-    d_gate = d_gated_ref[...] * att_hat * slope_ref[:, :WIDTH]
+    d_gate = d_gated_ref[:BLOCK, :] * att_hat * slope_ref[:, :WIDTH]
     d_query = collect(recv_ref, 2 * BLOCK, QUERIES)
     d_key = collect_sum(recv_ref, 0)
     d_normed = jnp.zeros((BLOCK, WIDTH), F32)
     for k, part in enumerate((d_gate, d_value, d_query, d_key)):
         d_normed += dot_nt(part.astype(BF16), proj_in_ref[:, k * WIDTH : (k + 1) * WIDTH])
     normed, inv_std = normalize(embedded_ref[...].astype(F32))
-    place = lax.axis_index("ctx") * BLOCK + iota((BLOCK, WIDTH), 0)
-    d_embedded = jnp.where(
-        place < length_ref[0],
-        upstream_ref[...].astype(F32) + norm_back(d_normed, normed, inv_std),
-        0.0,
-    ).astype(BF16)
-    in_head, in_first, in_second = place_masks(info_ref)
+    d_embedded = upstream_ref[...].astype(F32) + norm_back(d_normed, normed, inv_std)
+    d_embedded = jnp.where(valid, d_embedded, 0.0).astype(BF16)
+    in_head, in_first, in_second = place_masks(d_gated_ref)
     half = WIDTH // 2
     out_ref[:, :WIDTH] = dot(in_head, d_embedded).astype(BF16)
     out_ref[:, WIDTH:] = (
@@ -318,54 +336,37 @@
     ).astype(BF16)
 
 
-def output_kernel(length_ref, att_hat_ref, gate_ref, embedded_ref, proj_out_ref, out_ref):
-    gated = (att_hat_ref[...] * gate_ref[...].astype(F32)).astype(BF16)
-    total = embedded_ref[...].astype(F32) + dot(gated, proj_out_ref[...])
-    place = lax.axis_index("ctx") * BLOCK + iota((BLOCK, WIDTH), 0)
-    out_ref[...] = jnp.where(place < length_ref[0], total, 0.0).astype(BF16)
-
-
-def scatter_kernel(asked_ref, arrived_ref, out_ref):
-    head, tail = spread(asked_ref[...])
-    head_across = head.astype(F32).T
-    tail_across = tail.astype(F32).T
+def scatter_kernel(wanted_ref, arrived_ref, out_ref):
     half = WIDTH // 2
-    first = (iota((BLOCK, SENT), 1) & 7) < 4
-    rows = (iota((BLOCK, SENT), 0) + 1).astype(F32)
-    main = arrived_ref[:, :WIDTH]
     rest = arrived_ref[:, WIDTH:]
-    for k in range(SHARD_ROWS // BLOCK):
-        here = rows + float(BLOCK * k)
-        hot_head = one_hot(head_across == here)
-        in_tail = tail_across == here
-        total = dot(hot_head, main)
-        out = slice(k * BLOCK, (k + 1) * BLOCK)
-        out_ref[out, :half] = (total[:, :half] + dot(one_hot(in_tail & first), rest)).astype(BF16)
-        out_ref[out, half:] = (
-            total[:, half:] + dot(one_hot(in_tail & jnp.logical_not(first)), rest)
-        ).astype(BF16)
-
-
-def sum_kernel(parts_ref, out_ref):
+    row = (iota((SHARD_ROWS, SENT), 0) + 1).astype(F32)
+    total = dot(one_hot(row == wanted_ref[0:1, :]), arrived_ref[:, :WIDTH])
+    for k, start in enumerate((0, half)):
+        tail = dot(one_hot(row == wanted_ref[k + 1 : k + 2, :]), rest)
+        out_ref[:, start : start + half] = (total[:, start : start + half] + tail).astype(BF16)
+
+
+def output_kernel(parts_ref, gated_ref, embedded_ref, proj_out_ref, grad_ref, out_ref):
+    output = embedded_ref[...].astype(F32) + dot(gated_ref[...], proj_out_ref[...])
+    out_ref[...] = output.astype(BF16)
     total = parts_ref[0].astype(F32)
     for k in range(1, GROUPS):
         total += parts_ref[k].astype(F32)
-    out_ref[...] = total
-
-
-SCALAR = pl.BlockSpec(memory_space=pltpu.SMEM)
+    grad_ref[...] = total
+
+
 WHOLE = pl.BlockSpec(memory_space=pltpu.VMEM)
 
 
-def run(kernel, name, outs, *args, scalars=0, scratch=()):
+def run(kernel, name, outs, *args, scratch=(), vmem=40):
     single = not isinstance(outs, (list, tuple))
     return pl.pallas_call(
         kernel,
         out_shape=outs,
-        in_specs=[SCALAR] * scalars + [WHOLE] * (len(args) - scalars),
+        in_specs=[WHOLE] * len(args),
         out_specs=WHOLE if single else [WHOLE] * len(outs),
         scratch_shapes=scratch,
-        compiler_params=pltpu.CompilerParams(vmem_limit_bytes=40 * 1024 * 1024),
+        compiler_params=pltpu.CompilerParams(vmem_limit_bytes=vmem * 1024 * 1024),
         name=name,
     )(*args)
 
@@ -385,23 +386,25 @@
     requests, info = run(
         index_kernel,
         "index",
-        [shape(SENT, BLOCK, dtype=jnp.int32), shape(8, BLOCK, dtype=jnp.int32)],
-        history_len,
+        [shape(TABLES, BLOCK, dtype=jnp.int32), shape(8, BLOCK, dtype=jnp.int32)],
+        history_len.reshape(1, 1),
         item_ids,
         item_slot.reshape(BLOCK, BLOCK),
-        scalars=1,
-    )
-    asked = swap(requests.reshape(TABLES, MAIN, BLOCK), "table").reshape(SENT, BLOCK)
-    d_gated = run(
-        cotangent_kernel,
-        "cotangent",
-        shape(BLOCK, WIDTH, dtype=F32),
-        history_len,
+        vmem=60,
+    )
+    asked = swap(requests.reshape(TABLES, 1, BLOCK), "table")
+    slab, d_gated = run(
+        prepare_kernel,
+        "prepare",
+        [shape(SHARD_ROWS, WIDTH), shape(BLOCK + 8, WIDTH, dtype=F32)],
+        table_slab,
+        info,
         upstream,
         proj_out,
-        scalars=1,
-    )
-    rows_out = run(gather_kernel, "gather", shape(SENT, PACKED), asked, table_slab)
+    )
+    rows_out, wanted = run(
+        gather_kernel, "gather", [shape(SENT, PACKED), shape(8, SENT, dtype=F32)], asked, slab
+    )
     rows = swap(rows_out.reshape(TABLES, MAIN, PACKED), "table").reshape(SENT, PACKED)
     send, embedded, gate, slope = run(
         project_kernel,
@@ -412,7 +415,6 @@
             shape(BLOCK, WIDTH),
             shape(BLOCK, 2 * WIDTH, dtype=F32),
         ],
-        info,
         rows,
         proj_in,
         d_gated,
@@ -441,36 +443,29 @@
         scratch=[pltpu.VMEM((HEAD_DIM, SPAN), F32)],
     )
     back = swap(send_back, "ctx")
-    outgoing, att_hat = run(
+    outgoing, gated = run(
         finish_kernel,
         "finish",
-        [shape(SENT, PACKED), shape(BLOCK, WIDTH, dtype=F32)],
-        history_len,
-        info,
+        [shape(SENT, PACKED), shape(BLOCK, WIDTH)],
         back,
         embedded,
+        gate,
         slope,
         d_gated,
         upstream,
         proj_in,
-        scalars=1,
     )
     arrived = swap(outgoing.reshape(TABLES, MAIN, PACKED), "table").reshape(SENT, PACKED)
-    layer_out = run(
+    sums = run(scatter_kernel, "scatter", shape(SHARD_ROWS, WIDTH), wanted, arrived)
+    parts = swap(sums.reshape(GROUPS, SHARD_ROWS // GROUPS, WIDTH), "ctx")
+    table_grad, layer_out = run(
         output_kernel,
         "output",
-        shape(BLOCK, WIDTH),
-        history_len,
-        att_hat,
-        gate,
+        [shape(SHARD_ROWS // GROUPS, WIDTH, dtype=F32), shape(BLOCK, WIDTH)],
+        parts,
+        gated,
         embedded,
         proj_out,
-        scalars=1,
-    )
-    sums = run(scatter_kernel, "scatter", shape(SHARD_ROWS, WIDTH), asked, arrived)
-    parts = swap(sums.reshape(GROUPS, SHARD_ROWS // GROUPS, WIDTH), "ctx")
-    table_grad = run(
-        sum_kernel, "total", shape(SHARD_ROWS // GROUPS, WIDTH, dtype=F32), parts
     )
     return (layer_out[None], table_grad)
 

time: 184 us -> 174 us (0.946)
  waiting for transfers between devices: 36.7 us -> 7.51 us
  blocking collectives: 121 us -> 134 us
  starting transfers between devices: 8.71 us -> 16.8 us
    all_to_all x2 -> x1, waiting for transfers between devices: 36.7 us -> 7.51 us  [swap(): lax.all_to_all(array, axis, split_axis=0, concat_axis=0, tiled=True, axis...]
    all_to_all x5 -> x6, blocking collectives: 121 us -> 134 us  [swap(): lax.all_to_all(array, axis, split_axis=0, concat_axis=0, tiled=True, axis...]
    all_to_all x2 -> x1, starting transfers between devices: 8.71 us -> 16.8 us  [swap(): lax.all_to_all(array, axis, split_axis=0, concat_axis=0, tiled=True, axis...]
    pallas_call x10 -> x9, Pallas kernels: 11.2 us -> 10.4 us  [run(): pl.pallas_call(kernel, out_shape=outs, in_specs=[WHOLE] * len(args), out_...]
    unnamed x18 -> x14, local copies, waits for them, and re-layouts: 4.29 us -> 3.87 us
  transfers between devices with their start and end apart: 2 -> 1, of which waited for: 2 -> 1; matrix products, arithmetic and copies ran while one was open for 0% -> 0% of each run, Pallas kernels for 1% -> 0%
where the time goes in v2:
time: 174 us
  blocking collectives  134 us (77%)
  starting transfers between devices  16.8 us (10%)
  Pallas kernels  10.4 us (6%)
  waiting for transfers between devices  7.51 us (4%)
  local copies, waits for them, and re-layouts  3.87 us (2%)
    all_to_all x6, blocking collectives, swap(): lax.all_to_all(array, axis, split_axis=0, concat_axis=0, tiled=True, axis...  134 us
    all_to_all x1, starting transfers between devices, swap(): lax.all_to_all(array, axis, split_axis=0, concat_axis=0, tiled=True, axis...  16.8 us
    pallas_call x9, Pallas kernels, run(): pl.pallas_call(kernel, out_shape=outs, in_specs=[WHOLE] * len(args), out_...  10.4 us
    all_to_all x1, waiting for transfers between devices, swap(): lax.all_to_all(array, axis, split_axis=0, concat_axis=0, tiled=True, axis...  7.51 us
    unnamed x14, local copies, waits for them, and re-layouts  3.87 us
  transfers between devices with their start and end apart: 1, of which 1 were waited for; matrix products, arithmetic and copies ran while one was open for 0% of the time, Pallas kernels for 0%

profile of v2, /device:TPU:1, one launch (start us, length us, event | category | flops | bytes accessed | tf_op | source)
XLA Modules:
  0.0 173.7 jit_solution(9073319825510156333)
XLA Ops:
  1.3 2.0 %index.1 = (s32[32,128]{1,0:T(8,128)}, s32[8,128]{1,0:T(8,128)}) custom-call(s32[1,1]{1,0:T(1,128)} %bitcast.10.length_ref, s32[1,128]{1,0:T(1,128)} %ids_ref.1, s32[128,128]{1,0:T(8,128)} %bitcast.18), custom_call_target="tpu_custom_call" | custom-call | tf_op jit(solution)/shard_map/index/pallas_call | solution.py:363
  3.2 16.8 %all-to-all-start = ((s32[32,1,128]{2,1,0:T(1,128)}), s32[32,1,128]{2,1,0:T(1,128)S(1)}, u32[]{:S(2)}, u32[]{:S(2)}) async-start(s32[32,1,128]{2,1,0:T(1,128)} %bitcast.19), calls=%async_computation | async-start | bytes 32768 | tf_op jit(solution)/shard_map/all_to_all | solution.py:379
  20.0 0.0 copy-start.1
  20.0 1.0 copy-done.1
  21.0 1.2 copy-done.3
  22.3 0.9 copy-done.4
  23.2 0.7 copy-done.6
  23.9 0.3 prepare.1
  24.2 7.5 %all-to-all-done.asked_ref = s32[32,1,128]{2,1,0:T(1,128)S(1)} async-done(((s32[32,1,128]{2,1,0:T(1,128)}), s32[32,1,128]{2,1,0:T(1,128)S(1)}, u32[]{:S(2)}, u32[]{:S(2)}) %all-to-all-start) | async-done | bytes 16416 | tf_op jit(solution)/shard_map/all_to_all | solution.py:379
  31.7 0.6 gather.1
  32.3 32.5 %all_to_all.35 = bf16[32,8,768]{2,1,0:T(8,128)(2,1)S(1)} all-to-all(bf16[32,8,768]{2,1,0:T(8,128)(2,1)S(1)} %bitcast.17), channel_id=1, replica_groups=mesh['table'=32,'ctx'=16] {'table'}, dimensions={0} | all-to-all | bytes 786432 | tf_op jit(solution)/shard_map/all_to_all | solution.py:379
  64.7 1.0 project.1
  65.7 25.9 %all_to_all.36.recv_ref = bf16[16,320,128]{2,1,0:T(8,128)(2,1)S(1)} all-to-all(bf16[16,320,128]{2,1,0:T(8,128)(2,1)S(1)} %get-tuple-element.25), channel_id=1, replica_groups=mesh['table'=32,'ctx'=16] {'ctx'}, dimensions={0} | all-to-all | bytes 2621440 | tf_op jit(solution)/shard_map/all_to_all | solution.py:379
  91.6 1.4 attend.1
  93.0 6.8 %all_to_all.37.stats_ref = f32[4,8,512]{2,1,0:T(8,128)S(1)} all-to-all(f32[4,8,512]{2,1,0:T(8,128)S(1)} %get-tuple-element.28), channel_id=1, replica_groups={{0,1,2,3},{4,5,6,7},{8,9,10,11},{12,13,14,15},{16,17,18,19},{20,21,22,2..., dimensions={0} | all-to-all | bytes 131072 | tf_op jit(solution)/shard_map/all_to_all | solution.py:379
  99.9 2.5 %backward.1 = bf16[16,320,128]{2,1,0:T(8,128)(2,1)S(1)} custom-call(bf16[16,320,128]{2,1,0:T(8,128)(2,1)S(1)} %all_to_all.36.recv_ref, f32[128,512]{1,0:T(8,128)S(1)} %get-tuple-element.26.att_ref, f32[128,512]{1,0:T(8,128)S(1)} %get-tuple-element.27.d_hat_ref, f32[4,8,512]{2,1,0:T(8,128)S(1)} %all_to_all.37.stats_ref), custom_call_target="tpu_custom_call" | custom-call | tf_op jit(solution)/shard_map/backward/pallas_call | solution.py:363
  102.3 0.0 copy-start.5
  102.4 19.9 %all_to_all.38.recv_ref = bf16[16,320,128]{2,1,0:T(8,128)(2,1)S(1)} all-to-all(bf16[16,320,128]{2,1,0:T(8,128)(2,1)S(1)} %backward.1), channel_id=1, replica_groups=mesh['table'=32,'ctx'=16] {'ctx'}, dimensions={0} | all-to-all | bytes 2621440 | tf_op jit(solution)/shard_map/all_to_all | solution.py:379
  122.3 1.3 finish.1
  123.6 0.0 copy-start.2
  123.7 35.5 %all_to_all.39 = bf16[32,8,768]{2,1,0:T(8,128)(2,1)S(1)} all-to-all(bf16[32,8,768]{2,1,0:T(8,128)(2,1)S(1)} %bitcast.16), channel_id=1, replica_groups=mesh['table'=32,'ctx'=16] {'table'}, dimensions={0} | all-to-all | bytes 786432 | tf_op jit(solution)/shard_map/all_to_all | solution.py:379
  159.1 0.4 scatter.1
  159.6 13.2 %all_to_all.40.parts_ref = bf16[16,32,512]{2,1,0:T(8,128)(2,1)S(1)} all-to-all(bf16[16,32,512]{2,1,0:T(8,128)(2,1)S(1)} %bitcast.11), channel_id=1, replica_groups=mesh['table'=32,'ctx'=16] {'ctx'}, dimensions={0} | all-to-all | bytes 1048576 | tf_op jit(solution)/shard_map/all_to_all | solution.py:379
  172.8 0.9 output.1
  (7 shorter events, 0.0 us)
Async XLA Ops:
  3.2 28.5 %all-to-all-start = ((s32[32,1,128]{2,1,0:T(1,128)}), s32[32,1,128]{2,1,0:T(1,128)S(1)}, u32[]{:S(2)}, u32[]{:S(2)}) async-start(s32[32,1,128]{2,1,0:T(1,128)} %bitcast.19), calls=%async_computation | async-start | bytes 32768 | tf_op jit(solution)/shard_map/all_to_all | solution.py:379
  20.0 1.0 copy-start.1
  21.0 1.2 copy-start.3
  22.3 0.9 copy-start.4
  23.2 0.7 copy-start.6
  23.9 40.9 %copy-start = (bf16[512,2048]{1,0:T(8,128)(2,1)S(1)}, bf16[512,2048]{1,0:T(8,128)(2,1)}, u32[]{:S(2)}) copy-start(bf16[512,2048]{1,0:T(8,128)(2,1)} %proj_in_ref.3) | copy-start | bytes 6291460
  102.3 20.0 %copy-start.5 = (bf16[1,128,512]{2,1,0:T(8,128)(2,1)S(1)}, bf16[1,128,512]{2,1,0:T(8,128)(2,1)}, u32[]{:S(2)}) copy-start(bf16[1,128,512]{2,1,0:T(8,128)(2,1)} %param.13) | copy-start | bytes 393220
  123.6 49.1 %copy-start.2 = (bf16[512,512]{1,0:T(8,128)(2,1)S(1)}, bf16[512,512]{1,0:T(8,128)(2,1)}, u32[]{:S(2)}) copy-start(bf16[512,512]{1,0:T(8,128)(2,1)} %proj_out_ref.3) | copy-start | bytes 1572868

commit v3 on v2

--- a/solution.py
+++ b/solution.py
@@ -79,7 +79,8 @@
     low = dot_tn((table & 127).astype(F32).astype(BF16), rows_hot)
     both = jnp.where(row == (ids & 127), high * 128.0 + low, 0.0)
     slots = jnp.sum(both, axis=0, keepdims=True).astype(jnp.int32)
-    owner = jnp.where(valid, slots >> 9, TABLES)
+    shard = slots >> 9
+    owner = jnp.where(valid, 2 * ((11 * (shard >> 1)) & 15) + (shard & 1), TABLES)
     wanted = (slots & (SHARD_ROWS - 1)) + 1
     owned = iota((TABLES, BLOCK), 0) == owner
     owned_hot = one_hot(owned)
@@ -383,6 +384,7 @@
 
 def local(item_ids, history_len, item_slot, table_slab, proj_in, proj_out, upstream):
     upstream = upstream[0]
+    order = [[2 * ((3 * (p // 2)) % 16) + p % 2 for p in range(TABLES)]]
     requests, info = run(
         index_kernel,
         "index",
@@ -392,7 +394,7 @@
         item_slot.reshape(BLOCK, BLOCK),
         vmem=60,
     )
-    asked = swap(requests.reshape(TABLES, 1, BLOCK), "table")
+    asked = swap(requests.reshape(TABLES, 1, BLOCK), "table", order)
     slab, d_gated = run(
         prepare_kernel,
         "prepare",
@@ -405,7 +407,7 @@
     rows_out, wanted = run(
         gather_kernel, "gather", [shape(SENT, PACKED), shape(8, SENT, dtype=F32)], asked, slab
     )
-    rows = swap(rows_out.reshape(TABLES, MAIN, PACKED), "table").reshape(SENT, PACKED)
+    rows = swap(rows_out.reshape(TABLES, MAIN, PACKED), "table", order).reshape(SENT, PACKED)
     send, embedded, gate, slope = run(
         project_kernel,
         "project",
@@ -455,7 +457,7 @@
         upstream,
         proj_in,
     )
-    arrived = swap(outgoing.reshape(TABLES, MAIN, PACKED), "table").reshape(SENT, PACKED)
+    arrived = swap(outgoing.reshape(TABLES, MAIN, PACKED), "table", order).reshape(SENT, PACKED)
     sums = run(scatter_kernel, "scatter", shape(SHARD_ROWS, WIDTH), wanted, arrived)
     parts = swap(sums.reshape(GROUPS, SHARD_ROWS // GROUPS, WIDTH), "ctx")
     table_grad, layer_out = run(

time: 174 us -> 172 us (0.989); the launches traced: 174 us -> 169 us
  blocking collectives: 134 us -> 129 us
    all_to_all x6, blocking collectives: 134 us -> 129 us  [swap(): lax.all_to_all(array, axis, split_axis=0, concat_axis=0, tiled=True, axis...]
where the time goes in v3:
time: 172 us; the launch traced here: 169 us
  blocking collectives  129 us (75%)
  starting transfers between devices  16.8 us (10%)
  Pallas kernels  10.4 us (6%)
  waiting for transfers between devices  7.5 us (4%)
  local copies, waits for them, and re-layouts  3.87 us (2%)
    all_to_all x6, blocking collectives, swap(): lax.all_to_all(array, axis, split_axis=0, concat_axis=0, tiled=True, axis...  129 us
    all_to_all x1, starting transfers between devices, swap(): lax.all_to_all(array, axis, split_axis=0, concat_axis=0, tiled=True, axis...  16.8 us
    pallas_call x9, Pallas kernels, run(): pl.pallas_call(kernel, out_shape=outs, in_specs=[WHOLE] * len(args), out_...  10.4 us
    all_to_all x1, waiting for transfers between devices, swap(): lax.all_to_all(array, axis, split_axis=0, concat_axis=0, tiled=True, axis...  7.5 us
    unnamed x14, local copies, waits for them, and re-layouts  3.87 us
  transfers between devices with their start and end apart: 1, of which 1 were waited for; matrix products, arithmetic and copies ran while one was open for 0% of the time, Pallas kernels for 0%

profile of v3, /device:TPU:1, one launch (start us, length us, event | category | flops | bytes accessed | tf_op | source)
XLA Modules:
  0.0 169.2 jit_solution(16235414521943212937)
XLA Ops:
  1.3 2.0 %index.1 = (s32[32,128]{1,0:T(8,128)}, s32[8,128]{1,0:T(8,128)}) custom-call(s32[1,1]{1,0:T(1,128)} %bitcast.10.length_ref, s32[1,128]{1,0:T(1,128)} %ids_ref.1, s32[128,128]{1,0:T(8,128)} %bitcast.18), custom_call_target="tpu_custom_call" | custom-call | tf_op jit(solution)/shard_map/index/pallas_call | solution.py:364
  3.2 16.8 %all-to-all-start = ((s32[32,1,128]{2,1,0:T(1,128)}), s32[32,1,128]{2,1,0:T(1,128)S(1)}, u32[]{:S(2)}, u32[]{:S(2)}) async-start(s32[32,1,128]{2,1,0:T(1,128)} %bitcast.19), calls=%async_computation | async-start | bytes 32768 | tf_op jit(solution)/shard_map/all_to_all | solution.py:380
  20.0 0.0 copy-start.1
  20.0 1.0 copy-done.1
  21.0 1.2 copy-done.3
  22.3 0.9 copy-done.4
  23.2 0.7 copy-done.6
  23.9 0.3 prepare.1
  24.2 7.5 %all-to-all-done.asked_ref = s32[32,1,128]{2,1,0:T(1,128)S(1)} async-done(((s32[32,1,128]{2,1,0:T(1,128)}), s32[32,1,128]{2,1,0:T(1,128)S(1)}, u32[]{:S(2)}, u32[]{:S(2)}) %all-to-all-start) | async-done | bytes 16416 | tf_op jit(solution)/shard_map/all_to_all | solution.py:380
  31.7 0.6 gather.1
  32.3 30.4 %all_to_all.35 = bf16[32,8,768]{2,1,0:T(8,128)(2,1)S(1)} all-to-all(bf16[32,8,768]{2,1,0:T(8,128)(2,1)S(1)} %bitcast.17), channel_id=1, replica_groups={{0,16,96,112,192,208,288,304,384,400,480,496,64,80,160,176,256,272,352,..., dimensions={0} | all-to-all | bytes 786432 | tf_op jit(solution)/shard_map/all_to_all | solution.py:380
  62.7 1.0 project.1
  63.7 23.9 %all_to_all.36.recv_ref = bf16[16,320,128]{2,1,0:T(8,128)(2,1)S(1)} all-to-all(bf16[16,320,128]{2,1,0:T(8,128)(2,1)S(1)} %get-tuple-element.25), channel_id=1, replica_groups=mesh['table'=32,'ctx'=16] {'ctx'}, dimensions={0} | all-to-all | bytes 2621440 | tf_op jit(solution)/shard_map/all_to_all | solution.py:380
  87.6 1.4 attend.1
  89.1 6.8 %all_to_all.37.stats_ref = f32[4,8,512]{2,1,0:T(8,128)S(1)} all-to-all(f32[4,8,512]{2,1,0:T(8,128)S(1)} %get-tuple-element.28), channel_id=1, replica_groups={{0,1,2,3},{4,5,6,7},{8,9,10,11},{12,13,14,15},{16,17,18,19},{20,21,22,2..., dimensions={0} | all-to-all | bytes 131072 | tf_op jit(solution)/shard_map/all_to_all | solution.py:380
  95.9 2.5 %backward.1 = bf16[16,320,128]{2,1,0:T(8,128)(2,1)S(1)} custom-call(bf16[16,320,128]{2,1,0:T(8,128)(2,1)S(1)} %all_to_all.36.recv_ref, f32[128,512]{1,0:T(8,128)S(1)} %get-tuple-element.26.att_ref, f32[128,512]{1,0:T(8,128)S(1)} %get-tuple-element.27.d_hat_ref, f32[4,8,512]{2,1,0:T(8,128)S(1)} %all_to_all.37.stats_ref), custom_call_target="tpu_custom_call" | custom-call | tf_op jit(solution)/shard_map/backward/pallas_call | solution.py:364
  98.4 0.0 copy-start.5
  98.4 18.2 %all_to_all.38.recv_ref = bf16[16,320,128]{2,1,0:T(8,128)(2,1)S(1)} all-to-all(bf16[16,320,128]{2,1,0:T(8,128)(2,1)S(1)} %backward.1), channel_id=1, replica_groups=mesh['table'=32,'ctx'=16] {'ctx'}, dimensions={0} | all-to-all | bytes 2621440 | tf_op jit(solution)/shard_map/all_to_all | solution.py:380
  116.6 1.3 finish.1
  117.9 0.0 copy-start.2
  118.0 38.1 %all_to_all.39 = bf16[32,8,768]{2,1,0:T(8,128)(2,1)S(1)} all-to-all(bf16[32,8,768]{2,1,0:T(8,128)(2,1)S(1)} %bitcast.16), channel_id=1, replica_groups={{0,16,96,112,192,208,288,304,384,400,480,496,64,80,160,176,256,272,352,..., dimensions={0} | all-to-all | bytes 786432 | tf_op jit(solution)/shard_map/all_to_all | solution.py:380
  156.1 0.4 scatter.1
  156.5 11.7 %all_to_all.40.parts_ref = bf16[16,32,512]{2,1,0:T(8,128)(2,1)S(1)} all-to-all(bf16[16,32,512]{2,1,0:T(8,128)(2,1)S(1)} %bitcast.11), channel_id=1, replica_groups=mesh['table'=32,'ctx'=16] {'ctx'}, dimensions={0} | all-to-all | bytes 1048576 | tf_op jit(solution)/shard_map/all_to_all | solution.py:380
  168.3 0.9 output.1
  (7 shorter events, 0.0 us)
Async XLA Ops:
  3.2 28.5 %all-to-all-start = ((s32[32,1,128]{2,1,0:T(1,128)}), s32[32,1,128]{2,1,0:T(1,128)S(1)}, u32[]{:S(2)}, u32[]{:S(2)}) async-start(s32[32,1,128]{2,1,0:T(1,128)} %bitcast.19), calls=%async_computation | async-start | bytes 32768 | tf_op jit(solution)/shard_map/all_to_all | solution.py:380
  20.0 1.0 copy-start.1
  21.0 1.2 copy-start.3
  22.3 0.9 copy-start.4
  23.2 0.7 copy-start.6
  23.9 38.9 %copy-start = (bf16[512,2048]{1,0:T(8,128)(2,1)S(1)}, bf16[512,2048]{1,0:T(8,128)(2,1)}, u32[]{:S(2)}) copy-start(bf16[512,2048]{1,0:T(8,128)(2,1)} %proj_in_ref.3) | copy-start | bytes 6291460
  98.4 18.3 %copy-start.5 = (bf16[1,128,512]{2,1,0:T(8,128)(2,1)S(1)}, bf16[1,128,512]{2,1,0:T(8,128)(2,1)}, u32[]{:S(2)}) copy-start(bf16[1,128,512]{2,1,0:T(8,128)(2,1)} %param.13) | copy-start | bytes 393220
  117.9 50.3 %copy-start.2 = (bf16[512,512]{1,0:T(8,128)(2,1)S(1)}, bf16[512,512]{1,0:T(8,128)(2,1)}, u32[]{:S(2)}) copy-start(bf16[512,512]{1,0:T(8,128)(2,1)} %proj_out_ref.3) | copy-start | bytes 1572868

commit v4 on v3

--- a/solution.py
+++ b/solution.py
@@ -21,6 +21,8 @@
 MAIN = 8
 SENT = TABLES * MAIN
 PACKED = WIDTH + WIDTH // 2
+ORDER = [0, 1, 2, 3, 7, 6, 5, 4, 8, 9, 10, 11, 15, 14, 13, 12]
+PLACE = [ORDER.index(c) for c in range(GROUPS)]
 
 F32 = jnp.float32
 BF16 = jnp.bfloat16
@@ -179,7 +181,7 @@
         cols = slice(h * HEAD_DIM, (h + 1) * HEAD_DIM)
         for g in range(HEADS):
             rows = slice(g * QUERIES, (g + 1) * QUERIES)
-            chunk = HEADS * g + h
+            chunk = PLACE[HEADS * g + h]
             send_ref[chunk, 0:BLOCK, :] = key[:, cols]
             send_ref[chunk, BLOCK : 2 * BLOCK, :] = value[:, cols]
             send_ref[chunk, 2 * BLOCK : 2 * BLOCK + QUERIES, :] = query[rows, cols]
@@ -193,15 +195,17 @@
     return iota((SPAN, BLOCK), 0) <= place
 
 
+def take(recv_ref, blocks, first, rows):
+    return jnp.concatenate([recv_ref[PLACE[c], first : first + rows, :] for c in blocks], axis=0)
+
+
 def span_keys(recv_ref, j):
-    chunks = slice(4 * j, 4 * j + 4)
-    key = recv_ref[chunks, 0:BLOCK, :].reshape(SPAN, HEAD_DIM)
-    value = recv_ref[chunks, BLOCK : 2 * BLOCK, :].reshape(SPAN, HEAD_DIM)
-    return key, value
+    blocks = range(4 * j, 4 * j + 4)
+    return take(recv_ref, blocks, 0, BLOCK), take(recv_ref, blocks, BLOCK, BLOCK)
 
 
 def attend_kernel(recv_ref, att_ref, d_hat_ref, stats_ref):
-    query = recv_ref[:, 2 * BLOCK : 2 * BLOCK + QUERIES, :].reshape(SPAN, HEAD_DIM)
+    query = take(recv_ref, range(GROUPS), 2 * BLOCK, QUERIES)
     mask = allowed_mask()
     for j in range(4):
         key, value = span_keys(recv_ref, j)
@@ -216,7 +220,7 @@
             att_ref[...] = part
         else:
             att_ref[:, start:] += part
-    d_hat = recv_ref[:, 2 * BLOCK + QUERIES :, :].reshape(SPAN, HEAD_DIM)
+    d_hat = take(recv_ref, range(GROUPS), 2 * BLOCK + QUERIES, QUERIES)
     d_hat = d_hat.astype(F32).T
     d_hat_ref[...] = d_hat
     att = att_ref[...]
@@ -233,7 +237,7 @@
 
 
 def backward_kernel(recv_ref, att_ref, d_hat_ref, stats_ref, send_ref, d_query_ref):
-    query = recv_ref[:, 2 * BLOCK : 2 * BLOCK + QUERIES, :].reshape(SPAN, HEAD_DIM)
+    query = take(recv_ref, range(GROUPS), 2 * BLOCK, QUERIES)
     mask = allowed_mask()
     stats = [stats_ref[k] for k in range(HEADS)]
 
@@ -277,19 +281,19 @@
             d_query_ref[:, start:] += part
         for k in range(4):
             rows = slice(k * BLOCK, (k + 1) * BLOCK)
-            send_ref[4 * j + k, 0:BLOCK, :] = d_key[rows]
-            send_ref[4 * j + k, BLOCK : 2 * BLOCK, :] = d_value[rows]
+            send_ref[PLACE[4 * j + k], 0:BLOCK, :] = d_key[rows]
+            send_ref[PLACE[4 * j + k], BLOCK : 2 * BLOCK, :] = d_value[rows]
     d_query = d_query_ref[...].T.astype(BF16)
     for c in range(GROUPS):
         rows = slice(c * QUERIES, (c + 1) * QUERIES)
-        send_ref[c, 2 * BLOCK : 2 * BLOCK + QUERIES, :] = d_query[rows]
-        send_ref[c, 2 * BLOCK + QUERIES :, :] = out_att[rows]
+        send_ref[PLACE[c], 2 * BLOCK : 2 * BLOCK + QUERIES, :] = d_query[rows]
+        send_ref[PLACE[c], 2 * BLOCK + QUERIES :, :] = out_att[rows]
 
 
 def collect(recv_ref, first, rows):
     return jnp.concatenate(
         [
-            jnp.concatenate([recv_ref[HEADS * g + h, first : first + rows, :] for g in range(HEADS)], axis=0)
+            jnp.concatenate([recv_ref[PLACE[HEADS * g + h], first : first + rows, :] for g in range(HEADS)], axis=0)
             for h in range(HEADS)
         ],
         axis=1,
@@ -299,7 +303,7 @@
 def collect_sum(recv_ref, first):
     def head(h):
         return sum(
-            recv_ref[HEADS * g + h, first : first + BLOCK, :].astype(F32) for g in range(HEADS)
+            recv_ref[PLACE[HEADS * g + h], first : first + BLOCK, :].astype(F32) for g in range(HEADS)
         )
 
     return jnp.concatenate([head(h) for h in range(HEADS)], axis=1)
@@ -421,7 +425,7 @@
         proj_in,
         d_gated,
     )
-    recv = swap(send, "ctx")
+    recv = swap(send, "ctx", [ORDER])
     att, d_hat, stats = run(
         attend_kernel,
         "attend",
@@ -444,7 +448,7 @@
         stats,
         scratch=[pltpu.VMEM((HEAD_DIM, SPAN), F32)],
     )
-    back = swap(send_back, "ctx")
+    back = swap(send_back, "ctx", [ORDER])
     outgoing, gated = run(
         finish_kernel,
         "finish",

time: 172 us -> 171 us (level)
  no operation moved by 1% of the time
where the time goes in v4:
time: 171 us; the launch traced here: 168 us
  blocking collectives  129 us (75%)
  starting transfers between devices  16.8 us (10%)
  Pallas kernels  10.4 us (6%)
  waiting for transfers between devices  7.5 us (4%)
  local copies, waits for them, and re-layouts  3.87 us (2%)
    all_to_all x6, blocking collectives, swap(): lax.all_to_all(array, axis, split_axis=0, concat_axis=0, tiled=True, axis...  129 us
    all_to_all x1, starting transfers between devices, swap(): lax.all_to_all(array, axis, split_axis=0, concat_axis=0, tiled=True, axis...  16.8 us
    pallas_call x9, Pallas kernels, run(): pl.pallas_call(kernel, out_shape=outs, in_specs=[WHOLE] * len(args), out_...  10.4 us
    all_to_all x1, waiting for transfers between devices, swap(): lax.all_to_all(array, axis, split_axis=0, concat_axis=0, tiled=True, axis...  7.5 us
    unnamed x14, local copies, waits for them, and re-layouts  3.87 us
  transfers between devices with their start and end apart: 1, of which 1 were waited for; matrix products, arithmetic and copies ran while one was open for 0% of the time, Pallas kernels for 0%

profile of v4, /device:TPU:1, one launch (start us, length us, event | category | flops | bytes accessed | tf_op | source)
XLA Modules:
  0.0 168.4 jit_solution(10140051767204176118)
XLA Ops:
  1.3 2.0 %index.1 = (s32[32,128]{1,0:T(8,128)}, s32[8,128]{1,0:T(8,128)}) custom-call(s32[1,1]{1,0:T(1,128)} %bitcast.10.length_ref, s32[1,128]{1,0:T(1,128)} %ids_ref.1, s32[128,128]{1,0:T(8,128)} %bitcast.18), custom_call_target="tpu_custom_call" | custom-call | tf_op jit(solution)/shard_map/index/pallas_call | solution.py:368
  3.2 16.8 %all-to-all-start = ((s32[32,1,128]{2,1,0:T(1,128)}), s32[32,1,128]{2,1,0:T(1,128)S(1)}, u32[]{:S(2)}, u32[]{:S(2)}) async-start(s32[32,1,128]{2,1,0:T(1,128)} %bitcast.19), calls=%async_computation | async-start | bytes 32768 | tf_op jit(solution)/shard_map/all_to_all | solution.py:384
  20.0 0.0 copy-start.1
  20.0 1.0 copy-done.1
  21.0 1.2 copy-done.3
  22.3 0.9 copy-done.4
  23.2 0.7 copy-done.6
  23.9 0.3 prepare.1
  24.2 7.5 %all-to-all-done.asked_ref = s32[32,1,128]{2,1,0:T(1,128)S(1)} async-done(((s32[32,1,128]{2,1,0:T(1,128)}), s32[32,1,128]{2,1,0:T(1,128)S(1)}, u32[]{:S(2)}, u32[]{:S(2)}) %all-to-all-start) | async-done | bytes 16416 | tf_op jit(solution)/shard_map/all_to_all | solution.py:384
  31.7 0.6 gather.1
  32.3 30.4 %all_to_all.35 = bf16[32,8,768]{2,1,0:T(8,128)(2,1)S(1)} all-to-all(bf16[32,8,768]{2,1,0:T(8,128)(2,1)S(1)} %bitcast.17), channel_id=1, replica_groups={{0,16,96,112,192,208,288,304,384,400,480,496,64,80,160,176,256,272,352,..., dimensions={0} | all-to-all | bytes 786432 | tf_op jit(solution)/shard_map/all_to_all | solution.py:384
  62.7 1.0 project.1
  63.7 22.9 %all_to_all.36.recv_ref = bf16[16,320,128]{2,1,0:T(8,128)(2,1)S(1)} all-to-all(bf16[16,320,128]{2,1,0:T(8,128)(2,1)S(1)} %get-tuple-element.25), channel_id=1, replica_groups={{0,1,2,3,7,6,5,4,8,9,10,11,15,14,13,12},{16,17,18,19,23,22,21,20,24,25,..., dimensions={0} | all-to-all | bytes 2621440 | tf_op jit(solution)/shard_map/all_to_all | solution.py:384
  86.6 1.4 attend.1
  88.0 7.9 %all_to_all.37.stats_ref = f32[4,8,512]{2,1,0:T(8,128)S(1)} all-to-all(f32[4,8,512]{2,1,0:T(8,128)S(1)} %get-tuple-element.28), channel_id=1, replica_groups={{0,1,2,3},{4,5,6,7},{8,9,10,11},{12,13,14,15},{16,17,18,19},{20,21,22,2..., dimensions={0} | all-to-all | bytes 131072 | tf_op jit(solution)/shard_map/all_to_all | solution.py:384
  95.9 2.5 %backward.1 = bf16[16,320,128]{2,1,0:T(8,128)(2,1)S(1)} custom-call(bf16[16,320,128]{2,1,0:T(8,128)(2,1)S(1)} %all_to_all.36.recv_ref, f32[128,512]{1,0:T(8,128)S(1)} %get-tuple-element.26.att_ref, f32[128,512]{1,0:T(8,128)S(1)} %get-tuple-element.27.d_hat_ref, f32[4,8,512]{2,1,0:T(8,128)S(1)} %all_to_all.37.stats_ref), custom_call_target="tpu_custom_call" | custom-call | tf_op jit(solution)/shard_map/backward/pallas_call | solution.py:368
  98.4 0.0 copy-start.5
  98.4 18.6 %all_to_all.38.recv_ref = bf16[16,320,128]{2,1,0:T(8,128)(2,1)S(1)} all-to-all(bf16[16,320,128]{2,1,0:T(8,128)(2,1)S(1)} %backward.1), channel_id=1, replica_groups={{0,1,2,3,7,6,5,4,8,9,10,11,15,14,13,12},{16,17,18,19,23,22,21,20,24,25,..., dimensions={0} | all-to-all | bytes 2621440 | tf_op jit(solution)/shard_map/all_to_all | solution.py:384
  117.0 1.3 finish.1
  118.3 0.0 copy-start.2
  118.3 36.4 %all_to_all.39 = bf16[32,8,768]{2,1,0:T(8,128)(2,1)S(1)} all-to-all(bf16[32,8,768]{2,1,0:T(8,128)(2,1)S(1)} %bitcast.16), channel_id=1, replica_groups={{0,16,96,112,192,208,288,304,384,400,480,496,64,80,160,176,256,272,352,..., dimensions={0} | all-to-all | bytes 786432 | tf_op jit(solution)/shard_map/all_to_all | solution.py:384
  154.7 0.4 scatter.1
  155.1 12.4 %all_to_all.40.parts_ref = bf16[16,32,512]{2,1,0:T(8,128)(2,1)S(1)} all-to-all(bf16[16,32,512]{2,1,0:T(8,128)(2,1)S(1)} %bitcast.11), channel_id=1, replica_groups=mesh['table'=32,'ctx'=16] {'ctx'}, dimensions={0} | all-to-all | bytes 1048576 | tf_op jit(solution)/shard_map/all_to_all | solution.py:384
  167.5 0.9 output.1
  (7 shorter events, 0.0 us)
Async XLA Ops:
  3.2 28.5 %all-to-all-start = ((s32[32,1,128]{2,1,0:T(1,128)}), s32[32,1,128]{2,1,0:T(1,128)S(1)}, u32[]{:S(2)}, u32[]{:S(2)}) async-start(s32[32,1,128]{2,1,0:T(1,128)} %bitcast.19), calls=%async_computation | async-start | bytes 32768 | tf_op jit(solution)/shard_map/all_to_all | solution.py:384
  20.0 1.0 copy-start.1
  21.0 1.2 copy-start.3
  22.3 0.9 copy-start.4
  23.2 0.7 copy-start.6
  23.9 38.9 %copy-start = (bf16[512,2048]{1,0:T(8,128)(2,1)S(1)}, bf16[512,2048]{1,0:T(8,128)(2,1)}, u32[]{:S(2)}) copy-start(bf16[512,2048]{1,0:T(8,128)(2,1)} %proj_in_ref.3) | copy-start | bytes 6291460
  98.4 18.6 %copy-start.5 = (bf16[1,128,512]{2,1,0:T(8,128)(2,1)S(1)}, bf16[1,128,512]{2,1,0:T(8,128)(2,1)}, u32[]{:S(2)}) copy-start(bf16[1,128,512]{2,1,0:T(8,128)(2,1)} %param.13) | copy-start | bytes 393220
  118.3 49.2 %copy-start.2 = (bf16[512,512]{1,0:T(8,128)(2,1)S(1)}, bf16[512,512]{1,0:T(8,128)(2,1)}, u32[]{:S(2)}) copy-start(bf16[512,512]{1,0:T(8,128)(2,1)} %proj_out_ref.3) | copy-start | bytes 1572868

commit v5 on v4

--- a/solution.py
+++ b/solution.py
@@ -82,7 +82,7 @@
     both = jnp.where(row == (ids & 127), high * 128.0 + low, 0.0)
     slots = jnp.sum(both, axis=0, keepdims=True).astype(jnp.int32)
     shard = slots >> 9
-    owner = jnp.where(valid, 2 * ((11 * (shard >> 1)) & 15) + (shard & 1), TABLES)
+    owner = jnp.where(valid, 2 * (4 * ((((shard >> 1) & 3) - (3 - ((shard >> 1) >> 2))) & 3) + 3 - ((shard >> 1) >> 2)) + (shard & 1), TABLES)
     wanted = (slots & (SHARD_ROWS - 1)) + 1
     owned = iota((TABLES, BLOCK), 0) == owner
     owned_hot = one_hot(owned)
@@ -210,12 +210,16 @@
     for j in range(4):
         key, value = span_keys(recv_ref, j)
         start = j * BLOCK
-        half = dot_nt(key, query[start:, :]) * (0.5 * SCALE)
-        weight = half + half * jnp.tanh(half)
-        weight = jnp.concatenate(
-            [jnp.where(mask, weight[:, :BLOCK], 0.0), weight[:, BLOCK:]], axis=1
-        ) if j < 3 else jnp.where(mask, weight, 0.0)
-        part = dot_tn(value, weight.astype(BF16))
+        parts = []
+        for k in range(0, SPAN, SPAN // 2):
+            rows = slice(k, k + SPAN // 2)
+            half = dot_nt(key[rows], query[start:, :]) * (0.5 * SCALE)
+            weight = half + half * jnp.tanh(half)
+            first = jnp.where(mask[rows], weight[:, :BLOCK], 0.0)
+            if j < 3:
+                first = jnp.concatenate([first, weight[:, BLOCK:]], axis=1)
+            parts.append(first.astype(BF16))
+        part = dot_tn(value, jnp.concatenate(parts, axis=0))
         if j == 0:
             att_ref[...] = part
         else:
@@ -229,9 +233,7 @@
     d_mean = jnp.mean(d_hat, axis=0, keepdims=True)
     spread_sum = jnp.sum(centre * centre, axis=0, keepdims=True)
     cross_sum = jnp.sum(centre * (d_hat - d_mean), axis=0, keepdims=True)
-    rows = jnp.concatenate(
-        [mean, spread_sum, d_mean, cross_sum, mean, spread_sum, d_mean, cross_sum], axis=0
-    )
+    rows = jnp.concatenate([mean, spread_sum, d_mean, cross_sum], axis=0)
     for k in range(HEADS):
         stats_ref[k] = rows
 
@@ -388,7 +390,7 @@
 
 def local(item_ids, history_len, item_slot, table_slab, proj_in, proj_out, upstream):
     upstream = upstream[0]
-    order = [[2 * ((3 * (p // 2)) % 16) + p % 2 for p in range(TABLES)]]
+    order = [[2 * (4 * (3 - (p // 2) % 4) + ((p // 2) // 4 + (p // 2) % 4) % 4) + p % 2 for p in range(TABLES)]]
     requests, info = run(
         index_kernel,
         "index",
@@ -432,7 +434,7 @@
         [
             shape(HEAD_DIM, SPAN, dtype=F32),
             shape(HEAD_DIM, SPAN, dtype=F32),
-            shape(HEADS, 8, SPAN, dtype=F32),
+            shape(HEADS, 4, SPAN, dtype=F32),
         ],
         recv,
     )

time: 171 us -> 168 us (0.982); the launches traced: 168 us -> 168 us
  waiting for transfers between devices: 7.5 us -> 2.66 us
  blocking collectives: 129 us -> 133 us
    all_to_all x1, waiting for transfers between devices: 7.5 us -> 2.66 us  [swap(): lax.all_to_all(array, axis, split_axis=0, concat_axis=0, tiled=True, axis...]
    all_to_all x6, blocking collectives: 129 us -> 133 us  [swap(): lax.all_to_all(array, axis, split_axis=0, concat_axis=0, tiled=True, axis...]
where the time goes in v5:
time: 168 us
  blocking collectives  133 us (79%)
  starting transfers between devices  17 us (10%)
  Pallas kernels  10.4 us (6%)
  local copies, waits for them, and re-layouts  3.87 us (2%)
  waiting for transfers between devices  2.66 us (2%)
    all_to_all x6, blocking collectives, swap(): lax.all_to_all(array, axis, split_axis=0, concat_axis=0, tiled=True, axis...  133 us
    all_to_all x1, starting transfers between devices, swap(): lax.all_to_all(array, axis, split_axis=0, concat_axis=0, tiled=True, axis...  17 us
    pallas_call x9, Pallas kernels, run(): pl.pallas_call(kernel, out_shape=outs, in_specs=[WHOLE] * len(args), out_...  10.4 us
    unnamed x14, local copies, waits for them, and re-layouts  3.87 us
  transfers between devices with their start and end apart: 1, of which 1 were waited for; matrix products, arithmetic and copies ran while one was open for 0% of the time, Pallas kernels for 0%

profile of v5, /device:TPU:1, one launch (start us, length us, event | category | flops | bytes accessed | tf_op | source)
XLA Modules:
  0.0 167.8 jit_solution(7354856577531428856)
XLA Ops:
  1.3 2.0 %index.1 = (s32[32,128]{1,0:T(8,128)}, s32[8,128]{1,0:T(8,128)}) custom-call(s32[1,1]{1,0:T(1,128)} %bitcast.10.length_ref, s32[1,128]{1,0:T(1,128)} %ids_ref.1, s32[128,128]{1,0:T(8,128)} %bitcast.18), custom_call_target="tpu_custom_call" | custom-call | tf_op jit(solution)/shard_map/index/pallas_call | solution.py:370
  3.2 17.0 %all-to-all-start = ((s32[32,1,128]{2,1,0:T(1,128)}), s32[32,1,128]{2,1,0:T(1,128)S(1)}, u32[]{:S(2)}, u32[]{:S(2)}) async-start(s32[32,1,128]{2,1,0:T(1,128)} %bitcast.19), calls=%async_computation | async-start | bytes 32768 | tf_op jit(solution)/shard_map/all_to_all | solution.py:386
  20.2 0.0 copy-start.1
  20.2 1.0 copy-done.1
  21.3 1.2 copy-done.3
  22.5 0.9 copy-done.4
  23.4 0.7 copy-done.6
  24.1 0.3 prepare.1
  24.4 2.7 %all-to-all-done.asked_ref = s32[32,1,128]{2,1,0:T(1,128)S(1)} async-done(((s32[32,1,128]{2,1,0:T(1,128)}), s32[32,1,128]{2,1,0:T(1,128)S(1)}, u32[]{:S(2)}, u32[]{:S(2)}) %all-to-all-start) | async-done | bytes 16416 | tf_op jit(solution)/shard_map/all_to_all | solution.py:386
  27.1 0.6 gather.1
  27.7 31.6 %all_to_all.35 = bf16[32,8,768]{2,1,0:T(8,128)(2,1)S(1)} all-to-all(bf16[32,8,768]{2,1,0:T(8,128)(2,1)S(1)} %bitcast.17), channel_id=1, replica_groups={{384,400,288,304,192,208,96,112,416,432,320,336,224,240,0,16,448,464,35..., dimensions={0} | all-to-all | bytes 786432 | tf_op jit(solution)/shard_map/all_to_all | solution.py:386
  59.2 1.0 project.1
  60.2 25.5 %all_to_all.36.recv_ref = bf16[16,320,128]{2,1,0:T(8,128)(2,1)S(1)} all-to-all(bf16[16,320,128]{2,1,0:T(8,128)(2,1)S(1)} %get-tuple-element.25), channel_id=1, replica_groups={{0,1,2,3,7,6,5,4,8,9,10,11,15,14,13,12},{16,17,18,19,23,22,21,20,24,25,..., dimensions={0} | all-to-all | bytes 2621440 | tf_op jit(solution)/shard_map/all_to_all | solution.py:386
  85.8 1.4 attend.1
  87.1 6.7 %all_to_all.37.stats_ref = f32[4,4,512]{2,1,0:T(4,128)S(1)} all-to-all(f32[4,4,512]{2,1,0:T(4,128)S(1)} %get-tuple-element.28), channel_id=1, replica_groups={{0,1,2,3},{4,5,6,7},{8,9,10,11},{12,13,14,15},{16,17,18,19},{20,21,22,2..., dimensions={0} | all-to-all | bytes 65536 | tf_op jit(solution)/shard_map/all_to_all | solution.py:386
  93.8 2.5 %backward.1 = bf16[16,320,128]{2,1,0:T(8,128)(2,1)S(1)} custom-call(bf16[16,320,128]{2,1,0:T(8,128)(2,1)S(1)} %all_to_all.36.recv_ref, f32[128,512]{1,0:T(8,128)S(1)} %get-tuple-element.26.att_ref, f32[128,512]{1,0:T(8,128)S(1)} %get-tuple-element.27.d_hat_ref, f32[4,4,512]{2,1,0:T(4,128)S(1)} %all_to_all.37.stats_ref), custom_call_target="tpu_custom_call" | custom-call | tf_op jit(solution)/shard_map/backward/pallas_call | solution.py:370
  96.2 0.0 copy-start.5
  96.2 19.6 %all_to_all.38.recv_ref = bf16[16,320,128]{2,1,0:T(8,128)(2,1)S(1)} all-to-all(bf16[16,320,128]{2,1,0:T(8,128)(2,1)S(1)} %backward.1), channel_id=1, replica_groups={{0,1,2,3,7,6,5,4,8,9,10,11,15,14,13,12},{16,17,18,19,23,22,21,20,24,25,..., dimensions={0} | all-to-all | bytes 2621440 | tf_op jit(solution)/shard_map/all_to_all | solution.py:386
  115.9 1.3 finish.1
  117.2 0.0 copy-start.2
  117.2 34.8 %all_to_all.39 = bf16[32,8,768]{2,1,0:T(8,128)(2,1)S(1)} all-to-all(bf16[32,8,768]{2,1,0:T(8,128)(2,1)S(1)} %bitcast.16), channel_id=1, replica_groups={{384,400,288,304,192,208,96,112,416,432,320,336,224,240,0,16,448,464,35..., dimensions={0} | all-to-all | bytes 786432 | tf_op jit(solution)/shard_map/all_to_all | solution.py:386
  152.0 0.4 scatter.1
  152.5 14.5 %all_to_all.40.parts_ref = bf16[16,32,512]{2,1,0:T(8,128)(2,1)S(1)} all-to-all(bf16[16,32,512]{2,1,0:T(8,128)(2,1)S(1)} %bitcast.11), channel_id=1, replica_groups=mesh['table'=32,'ctx'=16] {'ctx'}, dimensions={0} | all-to-all | bytes 1048576 | tf_op jit(solution)/shard_map/all_to_all | solution.py:386
  166.9 0.9 output.1
  (7 shorter events, 0.0 us)
Async XLA Ops:
  3.2 23.8 %all-to-all-start = ((s32[32,1,128]{2,1,0:T(1,128)}), s32[32,1,128]{2,1,0:T(1,128)S(1)}, u32[]{:S(2)}, u32[]{:S(2)}) async-start(s32[32,1,128]{2,1,0:T(1,128)} %bitcast.19), calls=%async_computation | async-start | bytes 32768 | tf_op jit(solution)/shard_map/all_to_all | solution.py:386
  20.2 1.0 copy-start.1
  21.3 1.2 copy-start.3
  22.5 0.9 copy-start.4
  23.4 0.7 copy-start.6
  24.1 35.1 %copy-start = (bf16[512,2048]{1,0:T(8,128)(2,1)S(1)}, bf16[512,2048]{1,0:T(8,128)(2,1)}, u32[]{:S(2)}) copy-start(bf16[512,2048]{1,0:T(8,128)(2,1)} %proj_in_ref.3) | copy-start | bytes 6291460
  96.2 19.6 %copy-start.5 = (bf16[1,128,512]{2,1,0:T(8,128)(2,1)S(1)}, bf16[1,128,512]{2,1,0:T(8,128)(2,1)}, u32[]{:S(2)}) copy-start(bf16[1,128,512]{2,1,0:T(8,128)(2,1)} %param.13) | copy-start | bytes 393220
  117.2 49.7 %copy-start.2 = (bf16[512,512]{1,0:T(8,128)(2,1)S(1)}, bf16[512,512]{1,0:T(8,128)(2,1)}, u32[]{:S(2)}) copy-start(bf16[512,512]{1,0:T(8,128)(2,1)} %proj_out_ref.3) | copy-start | bytes 1572868

commit v6 on v5

--- a/solution.py
+++ b/solution.py
@@ -82,7 +82,7 @@
     both = jnp.where(row == (ids & 127), high * 128.0 + low, 0.0)
     slots = jnp.sum(both, axis=0, keepdims=True).astype(jnp.int32)
     shard = slots >> 9
-    owner = jnp.where(valid, 2 * (4 * ((((shard >> 1) & 3) - (3 - ((shard >> 1) >> 2))) & 3) + 3 - ((shard >> 1) >> 2)) + (shard & 1), TABLES)
+    owner = jnp.where(valid, 2 * (4 * ((((shard >> 1) & 3) - 3 * (3 - ((shard >> 1) >> 2))) & 3) + 3 - ((shard >> 1) >> 2)) + (shard & 1), TABLES)
     wanted = (slots & (SHARD_ROWS - 1)) + 1
     owned = iota((TABLES, BLOCK), 0) == owner
     owned_hot = one_hot(owned)
@@ -390,7 +390,7 @@
 
 def local(item_ids, history_len, item_slot, table_slab, proj_in, proj_out, upstream):
     upstream = upstream[0]
-    order = [[2 * (4 * (3 - (p // 2) % 4) + ((p // 2) // 4 + (p // 2) % 4) % 4) + p % 2 for p in range(TABLES)]]
+    order = [[2 * (4 * (3 - (p // 2) % 4) + ((p // 2) // 4 + 3 * ((p // 2) % 4)) % 4) + p % 2 for p in range(TABLES)]]
     requests, info = run(
         index_kernel,
         "index",

time: 168 us -> 167 us (level)
  no operation moved by 1% of the time
where the time goes in v6:
time: 167 us
  blocking collectives  132 us (79%)
  starting transfers between devices  17 us (10%)
  Pallas kernels  10.4 us (6%)
  local copies, waits for them, and re-layouts  3.87 us (2%)
  waiting for transfers between devices  2.66 us (2%)
    all_to_all x6, blocking collectives, swap(): lax.all_to_all(array, axis, split_axis=0, concat_axis=0, tiled=True, axis...  132 us
    all_to_all x1, starting transfers between devices, swap(): lax.all_to_all(array, axis, split_axis=0, concat_axis=0, tiled=True, axis...  17 us
    pallas_call x9, Pallas kernels, run(): pl.pallas_call(kernel, out_shape=outs, in_specs=[WHOLE] * len(args), out_...  10.4 us
    unnamed x14, local copies, waits for them, and re-layouts  3.87 us
  transfers between devices with their start and end apart: 1, of which 1 were waited for; matrix products, arithmetic and copies ran while one was open for 0% of the time, Pallas kernels for 0%

profile of v6, /device:TPU:1, one launch (start us, length us, event | category | flops | bytes accessed | tf_op | source)
XLA Modules:
  0.0 166.9 jit_solution(6946954228171610806)
XLA Ops:
  1.3 2.0 %index.1 = (s32[32,128]{1,0:T(8,128)}, s32[8,128]{1,0:T(8,128)}) custom-call(s32[1,1]{1,0:T(1,128)} %bitcast.10.length_ref, s32[1,128]{1,0:T(1,128)} %ids_ref.1, s32[128,128]{1,0:T(8,128)} %bitcast.18), custom_call_target="tpu_custom_call" | custom-call | tf_op jit(solution)/shard_map/index/pallas_call | solution.py:370
  3.2 17.0 %all-to-all-start = ((s32[32,1,128]{2,1,0:T(1,128)}), s32[32,1,128]{2,1,0:T(1,128)S(1)}, u32[]{:S(2)}, u32[]{:S(2)}) async-start(s32[32,1,128]{2,1,0:T(1,128)} %bitcast.19), calls=%async_computation | async-start | bytes 32768 | tf_op jit(solution)/shard_map/all_to_all | solution.py:386
  20.3 0.0 copy-start.1
  20.3 1.0 copy-done.1
  21.3 1.2 copy-done.3
  22.6 0.9 copy-done.4
  23.5 0.7 copy-done.6
  24.2 0.3 prepare.1
  24.5 2.7 %all-to-all-done.asked_ref = s32[32,1,128]{2,1,0:T(1,128)S(1)} async-done(((s32[32,1,128]{2,1,0:T(1,128)}), s32[32,1,128]{2,1,0:T(1,128)S(1)}, u32[]{:S(2)}, u32[]{:S(2)}) %all-to-all-start) | async-done | bytes 16416 | tf_op jit(solution)/shard_map/all_to_all | solution.py:386
  27.2 0.6 gather.1
  27.7 32.3 %all_to_all.35 = bf16[32,8,768]{2,1,0:T(8,128)(2,1)S(1)} all-to-all(bf16[32,8,768]{2,1,0:T(8,128)(2,1)S(1)} %bitcast.17), channel_id=1, replica_groups={{384,400,352,368,192,208,32,48,416,432,256,272,224,240,64,80,448,464,28..., dimensions={0} | all-to-all | bytes 786432 | tf_op jit(solution)/shard_map/all_to_all | solution.py:386
  60.0 1.0 project.1
  61.0 24.2 %all_to_all.36.recv_ref = bf16[16,320,128]{2,1,0:T(8,128)(2,1)S(1)} all-to-all(bf16[16,320,128]{2,1,0:T(8,128)(2,1)S(1)} %get-tuple-element.25), channel_id=1, replica_groups={{0,1,2,3,7,6,5,4,8,9,10,11,15,14,13,12},{16,17,18,19,23,22,21,20,24,25,..., dimensions={0} | all-to-all | bytes 2621440 | tf_op jit(solution)/shard_map/all_to_all | solution.py:386
  85.3 1.4 attend.1
  86.6 6.7 %all_to_all.37.stats_ref = f32[4,4,512]{2,1,0:T(4,128)S(1)} all-to-all(f32[4,4,512]{2,1,0:T(4,128)S(1)} %get-tuple-element.28), channel_id=1, replica_groups={{0,1,2,3},{4,5,6,7},{8,9,10,11},{12,13,14,15},{16,17,18,19},{20,21,22,2..., dimensions={0} | all-to-all | bytes 65536 | tf_op jit(solution)/shard_map/all_to_all | solution.py:386
  93.3 2.5 %backward.1 = bf16[16,320,128]{2,1,0:T(8,128)(2,1)S(1)} custom-call(bf16[16,320,128]{2,1,0:T(8,128)(2,1)S(1)} %all_to_all.36.recv_ref, f32[128,512]{1,0:T(8,128)S(1)} %get-tuple-element.26.att_ref, f32[128,512]{1,0:T(8,128)S(1)} %get-tuple-element.27.d_hat_ref, f32[4,4,512]{2,1,0:T(4,128)S(1)} %all_to_all.37.stats_ref), custom_call_target="tpu_custom_call" | custom-call | tf_op jit(solution)/shard_map/backward/pallas_call | solution.py:370
  95.8 0.0 copy-start.5
  95.8 21.5 %all_to_all.38.recv_ref = bf16[16,320,128]{2,1,0:T(8,128)(2,1)S(1)} all-to-all(bf16[16,320,128]{2,1,0:T(8,128)(2,1)S(1)} %backward.1), channel_id=1, replica_groups={{0,1,2,3,7,6,5,4,8,9,10,11,15,14,13,12},{16,17,18,19,23,22,21,20,24,25,..., dimensions={0} | all-to-all | bytes 2621440 | tf_op jit(solution)/shard_map/all_to_all | solution.py:386
  117.3 1.3 finish.1
  118.6 0.0 copy-start.2
  118.6 33.7 %all_to_all.39 = bf16[32,8,768]{2,1,0:T(8,128)(2,1)S(1)} all-to-all(bf16[32,8,768]{2,1,0:T(8,128)(2,1)S(1)} %bitcast.16), channel_id=1, replica_groups={{384,400,352,368,192,208,32,48,416,432,256,272,224,240,64,80,448,464,28..., dimensions={0} | all-to-all | bytes 786432 | tf_op jit(solution)/shard_map/all_to_all | solution.py:386
  152.4 0.4 scatter.1
  152.8 13.1 %all_to_all.40.parts_ref = bf16[16,32,512]{2,1,0:T(8,128)(2,1)S(1)} all-to-all(bf16[16,32,512]{2,1,0:T(8,128)(2,1)S(1)} %bitcast.11), channel_id=1, replica_groups=mesh['table'=32,'ctx'=16] {'ctx'}, dimensions={0} | all-to-all | bytes 1048576 | tf_op jit(solution)/shard_map/all_to_all | solution.py:386
  165.9 0.9 output.1
  (7 shorter events, 0.0 us)
Async XLA Ops:
  3.2 23.9 %all-to-all-start = ((s32[32,1,128]{2,1,0:T(1,128)}), s32[32,1,128]{2,1,0:T(1,128)S(1)}, u32[]{:S(2)}, u32[]{:S(2)}) async-start(s32[32,1,128]{2,1,0:T(1,128)} %bitcast.19), calls=%async_computation | async-start | bytes 32768 | tf_op jit(solution)/shard_map/all_to_all | solution.py:386
  20.3 1.0 copy-start.1
  21.3 1.2 copy-start.3
  22.6 0.9 copy-start.4
  23.5 0.7 copy-start.6
  24.2 35.9 %copy-start = (bf16[512,2048]{1,0:T(8,128)(2,1)S(1)}, bf16[512,2048]{1,0:T(8,128)(2,1)}, u32[]{:S(2)}) copy-start(bf16[512,2048]{1,0:T(8,128)(2,1)} %proj_in_ref.3) | copy-start | bytes 6291460
  95.8 21.5 %copy-start.5 = (bf16[1,128,512]{2,1,0:T(8,128)(2,1)S(1)}, bf16[1,128,512]{2,1,0:T(8,128)(2,1)}, u32[]{:S(2)}) copy-start(bf16[1,128,512]{2,1,0:T(8,128)(2,1)} %param.13) | copy-start | bytes 393220
  118.6 47.3 %copy-start.2 = (bf16[512,512]{1,0:T(8,128)(2,1)S(1)}, bf16[512,512]{1,0:T(8,128)(2,1)}, u32[]{:S(2)}) copy-start(bf16[512,512]{1,0:T(8,128)(2,1)} %proj_out_ref.3) | copy-start | bytes 1572868

commit v7 on v6

--- a/solution.py
+++ b/solution.py
@@ -82,7 +82,8 @@
     both = jnp.where(row == (ids & 127), high * 128.0 + low, 0.0)
     slots = jnp.sum(both, axis=0, keepdims=True).astype(jnp.int32)
     shard = slots >> 9
-    owner = jnp.where(valid, 2 * (4 * ((((shard >> 1) & 3) - 3 * (3 - ((shard >> 1) >> 2))) & 3) + 3 - ((shard >> 1) >> 2)) + (shard & 1), TABLES)
+    turn = 4 * ((((shard >> 1) & 3) - 3 * (3 - ((shard >> 1) >> 2))) & 3) + 3 - ((shard >> 1) >> 2)
+    owner = jnp.where(valid, 2 * turn + ((shard + turn) & 1), TABLES)
     wanted = (slots & (SHARD_ROWS - 1)) + 1
     owned = iota((TABLES, BLOCK), 0) == owner
     owned_hot = one_hot(owned)
@@ -390,7 +391,7 @@
 
 def local(item_ids, history_len, item_slot, table_slab, proj_in, proj_out, upstream):
     upstream = upstream[0]
-    order = [[2 * (4 * (3 - (p // 2) % 4) + ((p // 2) // 4 + 3 * ((p // 2) % 4)) % 4) + p % 2 for p in range(TABLES)]]
+    order = [[2 * (4 * (3 - (p // 2) % 4) + ((p // 2) // 4 + 3 * ((p // 2) % 4)) % 4) + (p + p // 2) % 2 for p in range(TABLES)]]
     requests, info = run(
         index_kernel,
         "index",

time: 167 us -> 166 us (level)
  the two profiles are of different devices: /device:TPU:1 before, /device:TPU:2 now
where the time goes in v7:
time: 166 us; the launch traced here: 165 us
  blocking collectives  131 us (79%)
  starting transfers between devices  15.9 us (10%)
  Pallas kernels  10.4 us (6%)
  local copies, waits for them, and re-layouts  3.87 us (2%)
  waiting for transfers between devices  2.95 us (2%)
    all_to_all x6, blocking collectives, swap(): lax.all_to_all(array, axis, split_axis=0, concat_axis=0, tiled=True, axis...  131 us
    all_to_all x1, starting transfers between devices, swap(): lax.all_to_all(array, axis, split_axis=0, concat_axis=0, tiled=True, axis...  15.9 us
    pallas_call x9, Pallas kernels, run(): pl.pallas_call(kernel, out_shape=outs, in_specs=[WHOLE] * len(args), out_...  10.4 us
    unnamed x14, local copies, waits for them, and re-layouts  3.87 us
  transfers between devices with their start and end apart: 1, of which 1 were waited for; matrix products, arithmetic and copies ran while one was open for 0% of the time, Pallas kernels for 0%

profile of v7, /device:TPU:2, one launch (start us, length us, event | category | flops | bytes accessed | tf_op | source)
XLA Modules:
  0.0 165.1 jit_solution(6214132548285497490)
XLA Ops:
  1.3 2.0 %index.1 = (s32[32,128]{1,0:T(8,128)}, s32[8,128]{1,0:T(8,128)}) custom-call(s32[1,1]{1,0:T(1,128)} %bitcast.10.length_ref, s32[1,128]{1,0:T(1,128)} %ids_ref.1, s32[128,128]{1,0:T(8,128)} %bitcast.18), custom_call_target="tpu_custom_call" | custom-call | tf_op jit(solution)/shard_map/index/pallas_call | solution.py:371
  3.3 15.9 %all-to-all-start = ((s32[32,1,128]{2,1,0:T(1,128)}), s32[32,1,128]{2,1,0:T(1,128)S(1)}, u32[]{:S(2)}, u32[]{:S(2)}) async-start(s32[32,1,128]{2,1,0:T(1,128)} %bitcast.19), calls=%async_computation | async-start | bytes 32768 | tf_op jit(solution)/shard_map/all_to_all | solution.py:387
  19.2 0.0 copy-start.1
  19.2 1.0 copy-done.1
  20.2 1.2 copy-done.3
  21.5 0.9 copy-done.4
  22.4 0.7 copy-done.6
  23.1 0.3 prepare.1
  23.4 2.9 %all-to-all-done.asked_ref = s32[32,1,128]{2,1,0:T(1,128)S(1)} async-done(((s32[32,1,128]{2,1,0:T(1,128)}), s32[32,1,128]{2,1,0:T(1,128)S(1)}, u32[]{:S(2)}, u32[]{:S(2)}) %all-to-all-start) | async-done | bytes 16416 | tf_op jit(solution)/shard_map/all_to_all | solution.py:387
  26.3 0.6 gather.1
  26.9 32.3 %all_to_all.35 = bf16[32,8,768]{2,1,0:T(8,128)(2,1)S(1)} all-to-all(bf16[32,8,768]{2,1,0:T(8,128)(2,1)S(1)} %bitcast.17), channel_id=1, replica_groups={{384,400,368,352,192,208,48,32,416,432,272,256,224,240,80,64,448,464,30..., dimensions={0} | all-to-all | bytes 786432 | tf_op jit(solution)/shard_map/all_to_all | solution.py:387
  59.2 1.0 project.1
  60.2 21.9 %all_to_all.36.recv_ref = bf16[16,320,128]{2,1,0:T(8,128)(2,1)S(1)} all-to-all(bf16[16,320,128]{2,1,0:T(8,128)(2,1)S(1)} %get-tuple-element.25), channel_id=1, replica_groups={{0,1,2,3,7,6,5,4,8,9,10,11,15,14,13,12},{16,17,18,19,23,22,21,20,24,25,..., dimensions={0} | all-to-all | bytes 2621440 | tf_op jit(solution)/shard_map/all_to_all | solution.py:387
  82.1 1.4 attend.1
  83.5 8.0 %all_to_all.37.stats_ref = f32[4,4,512]{2,1,0:T(4,128)S(1)} all-to-all(f32[4,4,512]{2,1,0:T(4,128)S(1)} %get-tuple-element.28), channel_id=1, replica_groups={{0,1,2,3},{4,5,6,7},{8,9,10,11},{12,13,14,15},{16,17,18,19},{20,21,22,2..., dimensions={0} | all-to-all | bytes 65536 | tf_op jit(solution)/shard_map/all_to_all | solution.py:387
  91.4 2.5 %backward.1 = bf16[16,320,128]{2,1,0:T(8,128)(2,1)S(1)} custom-call(bf16[16,320,128]{2,1,0:T(8,128)(2,1)S(1)} %all_to_all.36.recv_ref, f32[128,512]{1,0:T(8,128)S(1)} %get-tuple-element.26.att_ref, f32[128,512]{1,0:T(8,128)S(1)} %get-tuple-element.27.d_hat_ref, f32[4,4,512]{2,1,0:T(4,128)S(1)} %all_to_all.37.stats_ref), custom_call_target="tpu_custom_call" | custom-call | tf_op jit(solution)/shard_map/backward/pallas_call | solution.py:371
  93.9 0.0 copy-start.5
  93.9 18.9 %all_to_all.38.recv_ref = bf16[16,320,128]{2,1,0:T(8,128)(2,1)S(1)} all-to-all(bf16[16,320,128]{2,1,0:T(8,128)(2,1)S(1)} %backward.1), channel_id=1, replica_groups={{0,1,2,3,7,6,5,4,8,9,10,11,15,14,13,12},{16,17,18,19,23,22,21,20,24,25,..., dimensions={0} | all-to-all | bytes 2621440 | tf_op jit(solution)/shard_map/all_to_all | solution.py:387
  112.8 1.3 finish.1
  114.1 0.0 copy-start.2
  114.1 35.8 %all_to_all.39 = bf16[32,8,768]{2,1,0:T(8,128)(2,1)S(1)} all-to-all(bf16[32,8,768]{2,1,0:T(8,128)(2,1)S(1)} %bitcast.16), channel_id=1, replica_groups={{384,400,368,352,192,208,48,32,416,432,272,256,224,240,80,64,448,464,30..., dimensions={0} | all-to-all | bytes 786432 | tf_op jit(solution)/shard_map/all_to_all | solution.py:387
  149.9 0.4 scatter.1
  150.4 13.7 %all_to_all.40.parts_ref = bf16[16,32,512]{2,1,0:T(8,128)(2,1)S(1)} all-to-all(bf16[16,32,512]{2,1,0:T(8,128)(2,1)S(1)} %bitcast.11), channel_id=1, replica_groups=mesh['table'=32,'ctx'=16] {'ctx'}, dimensions={0} | all-to-all | bytes 1048576 | tf_op jit(solution)/shard_map/all_to_all | solution.py:387
  164.1 0.9 output.1
  (7 shorter events, 0.0 us)
Async XLA Ops:
  3.3 23.1 %all-to-all-start = ((s32[32,1,128]{2,1,0:T(1,128)}), s32[32,1,128]{2,1,0:T(1,128)S(1)}, u32[]{:S(2)}, u32[]{:S(2)}) async-start(s32[32,1,128]{2,1,0:T(1,128)} %bitcast.19), calls=%async_computation | async-start | bytes 32768 | tf_op jit(solution)/shard_map/all_to_all | solution.py:387
  19.2 1.0 copy-start.1
  20.2 1.2 copy-start.3
  21.5 0.9 copy-start.4
  22.4 0.7 copy-start.6
  23.0 36.2 %copy-start = (bf16[512,2048]{1,0:T(8,128)(2,1)S(1)}, bf16[512,2048]{1,0:T(8,128)(2,1)}, u32[]{:S(2)}) copy-start(bf16[512,2048]{1,0:T(8,128)(2,1)} %proj_in_ref.3) | copy-start | bytes 6291460
  93.9 18.9 %copy-start.5 = (bf16[1,128,512]{2,1,0:T(8,128)(2,1)S(1)}, bf16[1,128,512]{2,1,0:T(8,128)(2,1)}, u32[]{:S(2)}) copy-start(bf16[1,128,512]{2,1,0:T(8,128)(2,1)} %param.13) | copy-start | bytes 393220
  114.1 50.0 %copy-start.2 = (bf16[512,512]{1,0:T(8,128)(2,1)S(1)}, bf16[512,512]{1,0:T(8,128)(2,1)}, u32[]{:S(2)}) copy-start(bf16[512,512]{1,0:T(8,128)(2,1)} %proj_out_ref.3) | copy-start | bytes 1572868
